TPU v7x, 32 devices: a whole 2x2x4 slice. The times are simulated.
32 devices in a mesh: slices: 2 (over y), modes: 4 (over z), half: 4 (over x, core).
Axes of the slice: x: 2, y: 2, z: 4, core: 2. Of those that a mesh axis runs over, the one named last changes fastest.
Arguments:
- stem_state: bfloat16 [2, 8, 4, 2, 128, 128], P(None, ('slices', 'modes'), 'half'), parts along dimension 1, may hold values from -6 to 6
- branch_mats: bfloat16 [4, 6, 2, 128, 128], replicated, may hold values from -1 to 1
- branch_modes: int32 [4, 6], replicated, may hold values from 0 to 1
- out_proj: bfloat16 [4, 2, 512, 256], P('half'), may hold values from -0.1875 to 0.1875
- groups: int32 [8, 4, 64, 1], P(('slices', 'modes'), 'half'), parts along dimension 0, may hold values from 0 to 3; in each aligned block of 64 rows (0 to 63, 64 to 127, ..., all dimensions but the last counted through in order) at most 16 rows name the same one
Outputs:
- amplitudes: bfloat16 [8, 4, 2, 64, 256], P(('slices', 'modes'), 'half'), parts along dimension 0
There are 2 independent parts, one for each index of `slices`. A program takes and returns all parts, laid end to end along the dimension named above; an argument that names none is the same for every part. Nothing has to cross between parts.
Inputs may be any that keep to these rules, and one draw needn't show every extreme that they name: `branch_modes`: 0: the branch contracts the fifth index b of the state, 1: the sixth index c. `groups`: the 64 rows of one device name one group at most 16 times, and some device names some group exactly 16 times.
All inputs are finite; a program needn't handle non-finite values.
Results may differ from a plain program's by a relative error of at most 0.025.
Values may be sent and summed in bfloat16 or wider, within the bound.
A program may use at most 64 MiB of HBM per device.

v0:
```python
import jax
import jax.numpy as jnp
from jax import lax
from jax.sharding import PartitionSpec as P


def widen(matrix):
    real_part = matrix[0]
    imag_part = matrix[1]
    return jnp.stack([jnp.stack([real_part, imag_part]), jnp.stack([-imag_part, real_part])])


def contract_first(state, wide):
    value = jnp.einsum("isbc,ijbd->jsdc", state, wide, preferred_element_type=jnp.float32)
    return value.astype(jnp.bfloat16)


def contract_second(state, wide):
    value = jnp.einsum("isbc,ijcd->jsbd", state, wide, preferred_element_type=jnp.float32)
    return value.astype(jnp.bfloat16)


def local(stem_state, branch_mats, branch_modes, out_proj, groups):
    slabs = stem_state.shape[3]
    inner = stem_state.shape[4]
    state = stem_state.reshape(2, slabs, inner, inner)
    legs_total = branch_mats.shape[0]
    branch_total = branch_mats.shape[1]
    peers = lax.axis_size("modes")
    width_part = inner // peers
    for leg in range(legs_total):

        def advance(branch, current):
            wide = widen(branch_mats[leg][branch])
            return lax.cond(
                branch_modes[leg][branch] == 0, contract_first, contract_second, current, wide
            )

        state = lax.fori_loop(0, branch_total, advance, state)
        pieces = state.reshape(2, slabs, inner, peers, width_part)
        pieces = jnp.transpose(pieces, (3, 0, 1, 2, 4)).reshape(peers, 2, slabs, inner * width_part)
        pieces = lax.all_to_all(pieces, "modes", split_axis=0, concat_axis=0, tiled=True)
        pieces = pieces.reshape(peers, 2, slabs, inner, width_part)
        state = jnp.transpose(pieces, (1, 2, 3, 0, 4)).reshape(2, slabs, inner, inner)
    stem_len = out_proj.shape[2]
    out_len = out_proj.shape[3]
    row_total = slabs * inner * inner // stem_len
    rows = state.reshape(2, row_total, stem_len)
    chosen = groups.reshape(row_total)
    piece = lax.all_gather(out_proj, "half", axis=0, tiled=True)
    wides = jax.vmap(widen)(piece)
    product = jnp.einsum("irk,gijkd->gjrd", rows, wides, preferred_element_type=jnp.float32)
    owners = jnp.arange(piece.shape[0], dtype=jnp.int32)
    keep = chosen[None, :] == owners[:, None]
    products = jnp.where(keep[:, None, :, None], product, 0.0)
    result = jnp.sum(products, axis=0).astype(jnp.bfloat16)
    return result.reshape(1, 1, 2, row_total, out_len)


def solution(mesh):
    placed = (
        P(None, ("slices", "modes"), "half", None, None, None),
        P(),
        P(),
        P("half", None, None, None),
        P(("slices", "modes"), "half", None, None),
    )
    return jax.shard_map(
        local,
        mesh=mesh,
        in_specs=placed,
        out_specs=P(("slices", "modes"), "half", None, None, None),
        check_vma=False,
    )
```

profile of v0, /device:TPU:0, one launch (start us, length us, event | category | flops | bytes accessed | tf_op | source)
XLA Modules:
  0.0 110.7 jit_solution(9360158346139735370)
XLA Ops:
  6.5 1.0 copy.75
  7.6 1.9 %copy.76 = bf16[4,6,2,128,128]{3,4,2,1,0:T(8,128)(2,1)S(1)} copy(bf16[4,6,2,128,128]{4,3,2,1,0:T(8,128)(2,1)} %param.22) | data formatting | bytes 3145728 | tf_op jit(solution)/shard_map/while | solution.py:39
  9.5 10.8 %while.52 = (s32[]{:T(128)}, bf16[2,2,128,128]{2,3,1,0:T(8,128)(2,1)S(1)}, s32[4,6]{1,0:T(4,128)S(1)}, bf16[4,6,2,128,128]{3,4,2,1,0:T(8,128)(2,1)S(1)}, s32[]{:T(128)}, /*index=5*/s32[]{:T(128)}, s32[]{}) while((s32[]{:T(128)}, bf16[2,2,128,128]{2,3,1,0:T(8,128)(2,1)S(1)}, s32[4,6]{1,0:T(4,128)S(1)}, ...), condition=%wide.region_3.0_spmd, body=%wide.region_0.0_spmd.sunk | while | flops 33767428 | bytes 2359491 | solution.py:39
  16.8 0.7 fusion.57
  20.6 1.2 %reshape.198 = bf16[4,2,2,4096]{3,2,1,0:T(2,128)(2,1)} reshape(bf16[4,2,2,128,32]{4,3,2,1,0:T(8,128)(2,1)S(1)} %bitcast.310) | data formatting | bytes 262144 | tf_op jit(solution)/shard_map/reshape | solution.py:41
  21.8 6.3 %all-to-all-start = ((bf16[4,2,2,4096]{3,2,1,0:T(2,128)(2,1)}), bf16[4,2,2,4096]{3,2,1,0:T(2,128)(2,1)S(1)}, u32[]{:S(2)}, u32[]{:S(2)}) async-start(bf16[4,2,2,4096]{3,2,1,0:T(2,128)(2,1)} %reshape.198), calls=%async_computation | async-start | bytes 262144 | tf_op jit(solution)/shard_map/all_to_all | solution.py:42
  28.1 6.1 %all-to-all-done = bf16[4,2,2,4096]{3,2,1,0:T(2,128)(2,1)S(1)} async-done(((bf16[4,2,2,4096]{3,2,1,0:T(2,128)(2,1)}), bf16[4,2,2,4096]{3,2,1,0:T(2,128)(2,1)S(1)}, u32[]{:S(2)}, u32[]{:S(2)}) %all-to-all-start) | async-done | bytes 131104 | tf_op jit(solution)/shard_map/all_to_all | solution.py:42
  34.7 10.6 %while.53 = (s32[]{:T(128)}, bf16[2,2,128,128]{2,3,1,0:T(8,128)(2,1)S(1)}, s32[4,6]{1,0:T(4,128)S(1)}, bf16[4,6,2,128,128]{3,4,2,1,0:T(8,128)(2,1)S(1)}, s32[]{:T(128)}, /*index=5*/s32[]{:T(128)}, s32[]{}) while((s32[]{:T(128)}, bf16[2,2,128,128]{2,3,1,0:T(8,128)(2,1)S(1)}, s32[4,6]{1,0:T(4,128)S(1)}, ...), condition=%wide.region_7.0_spmd, body=%wide.region_4.0_spmd.sunk | while | flops 33767428 | bytes 2359491 | solution.py:39
  38.2 0.7 fusion.59
  41.8 0.7 fusion.59
  45.6 1.2 %reshape.202 = bf16[4,2,2,4096]{3,2,1,0:T(2,128)(2,1)} reshape(bf16[4,2,2,128,32]{4,3,2,1,0:T(8,128)(2,1)S(1)} %bitcast.312) | data formatting | bytes 262144 | tf_op jit(solution)/shard_map/reshape | solution.py:41
  46.8 3.3 %all-to-all-start.1 = ((bf16[4,2,2,4096]{3,2,1,0:T(2,128)(2,1)}), bf16[4,2,2,4096]{3,2,1,0:T(2,128)(2,1)S(1)}, u32[]{:S(2)}, u32[]{:S(2)}) async-start(bf16[4,2,2,4096]{3,2,1,0:T(2,128)(2,1)} %reshape.202), calls=%async_computation.1 | async-start | bytes 262144 | tf_op jit(solution)/shard_map/all_to_all | solution.py:42
  50.1 5.9 %all-to-all-done.1 = bf16[4,2,2,4096]{3,2,1,0:T(2,128)(2,1)S(1)} async-done(((bf16[4,2,2,4096]{3,2,1,0:T(2,128)(2,1)}), bf16[4,2,2,4096]{3,2,1,0:T(2,128)(2,1)S(1)}, u32[]{:S(2)}, u32[]{:S(2)}) %all-to-all-start.1) | async-done | bytes 131104 | tf_op jit(solution)/shard_map/all_to_all | solution.py:42
  56.5 10.5 %while.54 = (s32[]{:T(128)}, bf16[2,2,128,128]{2,3,1,0:T(8,128)(2,1)S(1)}, s32[4,6]{1,0:T(4,128)S(1)}, bf16[4,6,2,128,128]{3,4,2,1,0:T(8,128)(2,1)S(1)}, s32[]{:T(128)}, /*index=5*/s32[]{:T(128)}, s32[]{}) while((s32[]{:T(128)}, bf16[2,2,128,128]{2,3,1,0:T(8,128)(2,1)S(1)}, s32[4,6]{1,0:T(4,128)S(1)}, ...), condition=%wide.region_11.0_spmd, body=%wide.region_8.0_spmd.sunk | while | flops 33767428 | bytes 2359491 | solution.py:39
  67.2 1.2 %reshape.206 = bf16[4,2,2,4096]{3,2,1,0:T(2,128)(2,1)} reshape(bf16[4,2,2,128,32]{4,3,2,1,0:T(8,128)(2,1)S(1)} %bitcast.314) | data formatting | bytes 262144 | tf_op jit(solution)/shard_map/reshape | solution.py:41
  68.4 3.3 %all-to-all-start.2 = ((bf16[4,2,2,4096]{3,2,1,0:T(2,128)(2,1)}), bf16[4,2,2,4096]{3,2,1,0:T(2,128)(2,1)S(1)}, u32[]{:S(2)}, u32[]{:S(2)}) async-start(bf16[4,2,2,4096]{3,2,1,0:T(2,128)(2,1)} %reshape.206), calls=%async_computation.2 | async-start | bytes 262144 | tf_op jit(solution)/shard_map/all_to_all | solution.py:42
  71.8 0.7 all-gather.2.cloned.1.call-update
  72.5 5.1 %all-to-all-done.2 = bf16[4,2,2,4096]{3,2,1,0:T(2,128)(2,1)S(1)} async-done(((bf16[4,2,2,4096]{3,2,1,0:T(2,128)(2,1)}), bf16[4,2,2,4096]{3,2,1,0:T(2,128)(2,1)S(1)}, u32[]{:S(2)}, u32[]{:S(2)}) %all-to-all-start.2) | async-done | bytes 131104 | tf_op jit(solution)/shard_map/all_to_all | solution.py:42
  78.1 9.8 %while.55 = (s32[]{:T(128)}, bf16[2,2,128,128]{2,3,1,0:T(8,128)(2,1)S(1)}, s32[4,6]{1,0:T(4,128)S(1)}, bf16[4,6,2,128,128]{3,4,2,1,0:T(8,128)(2,1)S(1)}, s32[]{:T(128)}, /*index=5*/s32[]{:T(128)}, s32[]{}) while((s32[]{:T(128)}, bf16[2,2,128,128]{2,3,1,0:T(8,128)(2,1)S(1)}, s32[4,6]{1,0:T(4,128)S(1)}, ...), condition=%wide.region_15.0_spmd, body=%wide.region_12.0_spmd.sunk | while | flops 33767428 | bytes 2359491 | solution.py:39
  88.1 1.2 %reshape.210 = bf16[4,2,2,4096]{3,2,1,0:T(2,128)(2,1)} reshape(bf16[4,2,2,128,32]{4,3,2,1,0:T(8,128)(2,1)S(1)} %bitcast.316) | data formatting | bytes 262144 | tf_op jit(solution)/shard_map/reshape | solution.py:41
  89.3 3.3 %all-to-all-start.3 = ((bf16[4,2,2,4096]{3,2,1,0:T(2,128)(2,1)}), bf16[4,2,2,4096]{3,2,1,0:T(2,128)(2,1)S(1)}, u32[]{:S(2)}, u32[]{:S(2)}) async-start(bf16[4,2,2,4096]{3,2,1,0:T(2,128)(2,1)} %reshape.210), calls=%async_computation.3 | async-start | bytes 262144 | tf_op jit(solution)/shard_map/all_to_all | solution.py:42
  92.6 5.9 %all-to-all-done.3 = bf16[4,2,2,4096]{3,2,1,0:T(2,128)(2,1)S(1)} async-done(((bf16[4,2,2,4096]{3,2,1,0:T(2,128)(2,1)}), bf16[4,2,2,4096]{3,2,1,0:T(2,128)(2,1)S(1)}, u32[]{:S(2)}, u32[]{:S(2)}) %all-to-all-start.3) | async-done | bytes 131104 | tf_op jit(solution)/shard_map/all_to_all | solution.py:42
  99.7 1.8 %slice_bitcast_fusion = (bf16[1,4,512,256]{3,2,0,1:T(8,128)(2,1)S(1)}, bf16[1,4,512,256]{3,2,0,1:T(8,128)(2,1)S(1)}) fusion(bf16[4,2,512,256]{3,2,0,1:T(8,128)(2,1)} %all-gather.2.cloned.1.call-done), kind=kLoop, calls=%fused_computation.73 | loop fusion | bytes 4194304 | tf_op jit(solution)/shard_map/vmap()/stack;vmap()/squeeze | solution.py:10
  102.4 1.5 %fusion.37 = bf16[2,256,64]{1,2,0:T(8,128)(2,1)} fusion(bf16[1,2,4,512,256]{4,3,0,1,2:T(8,128)(2,1)S(1)} %get-tuple-element.548, bf16[1,2,4,512,256]{4,3,0,1,2:T(8,128)(2,1)S(1)} %get-tuple-element.547, pred[4,64]{1,0:T(4,128)(4,1)S(1)} %iota_compare_fusion, bf16[2,64,512,1,1]{2,1,0,3,4:T(8,128)(2,1)S(1)} %reshape.240), kind=kOutput, calls=%fused_computation.72 | convolution fusion | flops 277053440 | bytes 4391168 | tf_op jit(solution)/shard_map/irk,gijkd->gjrd/dot_general | solution.py:52
  (273 shorter events, 34.0 us)
Async XLA Ops:
  6.5 3.0 %copy-start.1 = (s32[4,6]{1,0:T(4,128)S(1)}, s32[4,6]{1,0:T(4,128)}, u32[]{:S(2)}) copy-start(s32[4,6]{1,0:T(4,128)} %param.23) | copy-start | bytes 292
  21.8 12.4 %all-to-all-start = ((bf16[4,2,2,4096]{3,2,1,0:T(2,128)(2,1)}), bf16[4,2,2,4096]{3,2,1,0:T(2,128)(2,1)S(1)}, u32[]{:S(2)}, u32[]{:S(2)}) async-start(bf16[4,2,2,4096]{3,2,1,0:T(2,128)(2,1)} %reshape.198), calls=%async_computation | async-start | bytes 262144 | tf_op jit(solution)/shard_map/all_to_all | solution.py:42
  46.8 9.2 %all-to-all-start.1 = ((bf16[4,2,2,4096]{3,2,1,0:T(2,128)(2,1)}), bf16[4,2,2,4096]{3,2,1,0:T(2,128)(2,1)S(1)}, u32[]{:S(2)}, u32[]{:S(2)}) async-start(bf16[4,2,2,4096]{3,2,1,0:T(2,128)(2,1)} %reshape.202), calls=%async_computation.1 | async-start | bytes 262144 | tf_op jit(solution)/shard_map/all_to_all | solution.py:42
  68.4 9.2 %all-to-all-start.2 = ((bf16[4,2,2,4096]{3,2,1,0:T(2,128)(2,1)}), bf16[4,2,2,4096]{3,2,1,0:T(2,128)(2,1)S(1)}, u32[]{:S(2)}, u32[]{:S(2)}) async-start(bf16[4,2,2,4096]{3,2,1,0:T(2,128)(2,1)} %reshape.206), calls=%async_computation.2 | async-start | bytes 262144 | tf_op jit(solution)/shard_map/all_to_all | solution.py:42
  71.7 28.0 %all-gather.2.cloned.1.call-start = ((), (), s32[]{:S(2)}) async-start(), calls=%async_computation.4 | async-start | bytes 2621440 | tf_op jit(solution)/shard_map/all_gather | solution.py:50
  78.1 14.6 %copy-start.2 = (s32[1,1,64,1]{2,3,1,0:T(1,128)S(1)}, s32[1,1,64,1]{2,3,1,0:T(1,128)}, u32[]{:S(2)}) copy-start(s32[1,1,64,1]{2,3,1,0:T(1,128)} %param.25) | copy-start | bytes 772
  89.3 9.2 %all-to-all-start.3 = ((bf16[4,2,2,4096]{3,2,1,0:T(2,128)(2,1)}), bf16[4,2,2,4096]{3,2,1,0:T(2,128)(2,1)S(1)}, u32[]{:S(2)}, u32[]{:S(2)}) async-start(bf16[4,2,2,4096]{3,2,1,0:T(2,128)(2,1)} %reshape.210), calls=%async_computation.3 | async-start | bytes 262144 | tf_op jit(solution)/shard_map/all_to_all | solution.py:42
  99.7 2.2 %copy-start = (bf16[4,2,512,256]{3,2,0,1:T(8,128)(2,1)S(1)}, bf16[4,2,512,256]{3,2,0,1:T(8,128)(2,1)}, u32[]{:S(2)}) copy-start(bf16[4,2,512,256]{3,2,0,1:T(8,128)(2,1)} %all-gather.2.cloned.1.call-done) | copy-start | bytes 6291460
Sparse Core Ops, SparseCore 0:
  74.1 23.9 all-gather.1
where the time goes:
time: 111 us
  waiting for transfers between devices  23.7 us (21%)
  loops' own time  17.5 us (16%)
  other arithmetic  17 us (15%)
  local copies, waits for them, and re-layouts  16.3 us (15%)
  starting transfers between devices  16.3 us (15%)
  between operations  13.6 us (12%)
  matrix products  6.35 us (6%)
    all_to_all x4, waiting for transfers between devices, local(): lax.all_to_all(pieces, 'modes', split_axis=0, concat_axis=0, tiled=True)  23 us
    another operation x4, loops' own time, local(): state = lax.fori_loop(0, branch_total, advance, state)  16.8 us
    all_to_all x4, starting transfers between devices, local(): lax.all_to_all(pieces, 'modes', split_axis=0, concat_axis=0, tiled=True)  16.3 us
    eq x24, other arithmetic, advance(): branch_modes[leg][branch] == 0  15.4 us
    reshape x4, local copies, waits for them, and re-layouts, local(): jnp.transpose(pieces, (3, 0, 1, 2, 4))  4.66 us
    dot_general x12, matrix products, contract_first(): jnp.einsum('isbc,ijbd->jsdc', state, wide, preferred_element_type=jnp.flo...  2.63 us
    dot_general x12, matrix products, contract_second(): jnp.einsum('isbc,ijcd->jsbd', state, wide, preferred_element_type=jnp.flo...  2.24 us
  transfers between devices with their start and end apart: 5, of which 4 were waited for; matrix products, arithmetic and copies ran while one was open for 8% of the time, Pallas kernels for 0%

commit v1 on v0

--- a/solution.py
+++ b/solution.py
@@ -1,7 +1,14 @@
+import functools
+
 import jax
 import jax.numpy as jnp
 from jax import lax
+from jax.experimental import pallas as pl
+from jax.experimental.pallas import tpu as pltpu
 from jax.sharding import PartitionSpec as P
+
+MESH = pl.DeviceIdType.MESH
+CHUNKS = 4
 
 
 def widen(matrix):
@@ -20,15 +27,13 @@
     return value.astype(jnp.bfloat16)
 
 
-def local(stem_state, branch_mats, branch_modes, out_proj, groups):
+def stepwise(stem_state, branch_mats, branch_modes, out_proj, groups):
     slabs = stem_state.shape[3]
     inner = stem_state.shape[4]
     state = stem_state.reshape(2, slabs, inner, inner)
-    legs_total = branch_mats.shape[0]
-    branch_total = branch_mats.shape[1]
     peers = lax.axis_size("modes")
     width_part = inner // peers
-    for leg in range(legs_total):
+    for leg in range(branch_mats.shape[0]):
 
         def advance(branch, current):
             wide = widen(branch_mats[leg][branch])
@@ -36,7 +41,7 @@
                 branch_modes[leg][branch] == 0, contract_first, contract_second, current, wide
             )
 
-        state = lax.fori_loop(0, branch_total, advance, state)
+        state = lax.fori_loop(0, branch_mats.shape[1], advance, state)
         pieces = state.reshape(2, slabs, inner, peers, width_part)
         pieces = jnp.transpose(pieces, (3, 0, 1, 2, 4)).reshape(peers, 2, slabs, inner * width_part)
         pieces = lax.all_to_all(pieces, "modes", split_axis=0, concat_axis=0, tiled=True)
@@ -57,6 +62,362 @@
     return result.reshape(1, 1, 2, row_total, out_len)
 
 
+def dot(left, right):
+    return jnp.dot(left, right, preferred_element_type=jnp.float32)
+
+
+def wide_of(top):
+    inner = top.shape[0]
+    real_part, imag_part = top[:, :inner], top[:, inner:]
+    return jnp.concatenate([top, jnp.concatenate([-imag_part, real_part], axis=1)], axis=0)
+
+
+def normal(top):
+    largest = jnp.max(jnp.abs(top), axis=(0, 1), keepdims=True)
+    largest = jnp.where(largest > 0.0, largest, 1.0)
+    return top / largest, largest
+
+
+def fused(
+    sizes,
+    state_ref,
+    mats_hbm,
+    modes_ref,
+    proj_ref,
+    groups_ref,
+    out_ref,
+    mats,
+    got,
+    leave,
+    back,
+    weights,
+    local_sem,
+    first_send,
+    first_recv,
+    last_send,
+    last_recv,
+    x_send,
+    x_recv,
+    y_send,
+    y_recv,
+    core_send,
+    core_recv,
+):
+    peers, legs, branches, slabs, inner, depth = sizes
+    width = inner // peers
+    me = lax.axis_index("modes")
+    row = lax.axis_index("slices")
+    home = lax.axis_index("half")
+    core = lax.rem(home, 2)
+    sibling = home + 1 - 2 * core
+    across = lax.rem(home + 2, 4)
+    across_sibling = lax.rem(sibling + 2, 4)
+    other_row = 1 - row
+    part = got.shape[2]
+    half_depth = depth // 2
+    piece = half_depth // CHUNKS
+
+    load_mats = pltpu.make_async_copy(mats_hbm, mats, local_sem.at[0])
+    load_mats.start()
+    load_own = pltpu.make_async_copy(
+        state_ref.at[:, pl.ds(me * part, part), :], got.at[me], local_sem.at[1]
+    )
+    load_own.start()
+    load_proj = pltpu.make_async_copy(proj_ref, weights.at[home], local_sem.at[2])
+    load_proj.start()
+
+    barrier = pltpu.get_barrier_semaphore()
+    for step in range(1, peers):
+        pl.semaphore_signal(
+            barrier, inc=1, device_id={"modes": lax.rem(me + step, peers)}, device_id_type=MESH
+        )
+    pl.semaphore_signal(barrier, inc=1, device_id={"half": sibling}, device_id_type=MESH)
+    pl.semaphore_signal(barrier, inc=1, device_id={"half": across}, device_id_type=MESH)
+    pl.semaphore_signal(barrier, inc=1, device_id={"slices": other_row}, device_id_type=MESH)
+    pl.semaphore_wait(barrier, peers + 2)
+
+    first = []
+    for step in range(1, peers):
+        target = lax.rem(me + step, peers)
+        copy = pltpu.make_async_remote_copy(
+            src_ref=state_ref.at[:, pl.ds(target * part, part), :],
+            dst_ref=got.at[me],
+            send_sem=first_send.at[step - 1],
+            recv_sem=first_recv.at[step - 1],
+            device_id={"modes": target},
+            device_id_type=MESH,
+        )
+        copy.start()
+        first.append(copy)
+
+    def rows_of(which, chunk):
+        return pl.ds(which * half_depth + chunk * piece, piece)
+
+    over_x, over_y, over_core = [], [], []
+    for chunk in range(CHUNKS):
+        copy = pltpu.make_async_remote_copy(
+            src_ref=proj_ref.at[:, rows_of(row, chunk), :],
+            dst_ref=weights.at[home, :, rows_of(row, chunk), :],
+            send_sem=x_send.at[chunk],
+            recv_sem=x_recv.at[chunk],
+            device_id={"half": across},
+            device_id_type=MESH,
+        )
+        copy.start()
+        over_x.append(copy)
+    own = pltpu.make_async_remote_copy(
+        src_ref=proj_ref,
+        dst_ref=weights.at[home],
+        send_sem=core_send.at[0],
+        recv_sem=core_recv.at[0],
+        device_id={"half": sibling},
+        device_id_type=MESH,
+    )
+    own.start()
+
+    def to_core(which, chunk, number):
+        copy = pltpu.make_async_remote_copy(
+            src_ref=weights.at[across, :, rows_of(which, chunk), :],
+            dst_ref=weights.at[across, :, rows_of(which, chunk), :],
+            send_sem=core_send.at[number],
+            recv_sem=core_recv.at[number],
+            device_id={"half": sibling},
+            device_id_type=MESH,
+        )
+        copy.start()
+        over_core.append(copy)
+
+    def hand_on(chunk):
+        over_x[chunk].wait_recv()
+        copy = pltpu.make_async_remote_copy(
+            src_ref=weights.at[across, :, rows_of(row, chunk), :],
+            dst_ref=weights.at[across, :, rows_of(row, chunk), :],
+            send_sem=y_send.at[chunk],
+            recv_sem=y_recv.at[chunk],
+            device_id={"slices": other_row},
+            device_id_type=MESH,
+        )
+        copy.start()
+        over_y.append(copy)
+        to_core(row, chunk, 1 + chunk)
+
+    def take_in(chunk):
+        over_y[chunk].wait_recv()
+        to_core(other_row, chunk, 1 + CHUNKS + chunk)
+
+    load_mats.wait()
+    lanes = lax.broadcasted_iota(jnp.int32, (inner, 2 * inner), 1)
+    sublanes = lax.broadcasted_iota(jnp.int32, (inner, 2 * inner), 0)
+    identity = jnp.where(lanes == sublanes, 1.0, 0.0).astype(jnp.float32)
+    over_b, over_c = [], []
+    for leg in range(legs):
+        top = jnp.concatenate([mats[leg, 0, 0], mats[leg, 0, 1]], axis=1).astype(jnp.float32)
+        is_b = modes_ref[leg, 0] == 0
+        over_b.append(jnp.where(is_b, top, identity))
+        over_c.append(jnp.where(is_b, identity, top))
+    for branch in range(1, branches):
+        for leg in range(legs):
+            is_b = modes_ref[leg, branch] == 0
+            top = jnp.concatenate([mats[leg, branch, 0], mats[leg, branch, 1]], axis=1)
+            chosen = jnp.where(is_b, over_b[leg], over_c[leg]).astype(jnp.bfloat16)
+            value = dot(chosen, wide_of(top))
+            over_b[leg] = jnp.where(is_b, value, over_b[leg])
+            over_c[leg] = jnp.where(is_b, over_c[leg], value)
+    gains = []
+    wides = []
+    for leg in range(legs):
+        scaled, gain = normal(over_c[leg])
+        gains.append(gain)
+        wides.append(wide_of(scaled.astype(jnp.bfloat16)))
+        scaled, gain = normal(over_b[leg])
+        gains.append(gain)
+        over_b[leg] = scaled.astype(jnp.bfloat16)
+
+    load_own.wait()
+    for copy in first:
+        copy.wait()
+    values = jnp.concatenate(
+        [jnp.concatenate([got[m, 0], got[m, 1]], axis=1) for m in range(peers)], axis=0
+    )
+    block = lax.broadcasted_iota(jnp.int32, (part, inner), 1) // width
+    for leg in range(legs):
+        product = dot(values, wides[leg])
+        swapped = []
+        for m in range(peers):
+            both = []
+            for comp in range(2):
+                taken = None
+                for t in range(peers):
+                    tile = product[t * part : (t + 1) * part, comp * inner : (comp + 1) * inner]
+                    shift = (t - m) * width % inner
+                    if shift:
+                        tile = pltpu.roll(tile, shift, 1)
+                    taken = tile if taken is None else jnp.where(block == t, tile, taken)
+                both.append(taken)
+            swapped.append(jnp.concatenate(both, axis=1))
+        values = jnp.concatenate(swapped, axis=0).astype(jnp.bfloat16)
+    for m in range(peers):
+        leave[m] = values[m * part : (m + 1) * part]
+
+    last = []
+    for step in range(1, peers):
+        target = lax.rem(me + step, peers)
+        copy = pltpu.make_async_remote_copy(
+            src_ref=leave.at[target],
+            dst_ref=back.at[me],
+            send_sem=last_send.at[step - 1],
+            recv_sem=last_recv.at[step - 1],
+            device_id={"modes": target},
+            device_id_type=MESH,
+        )
+        copy.start()
+        last.append(copy)
+    back[me] = leave[me]
+    for chunk in range(CHUNKS):
+        hand_on(chunk)
+
+    total = over_b[0]
+    for leg in range(1, legs):
+        total = dot(total, wide_of(over_b[leg])).astype(jnp.bfloat16)
+    stacked = jnp.concatenate([total[:, :inner], total[:, inner:]], axis=0)
+    quad = depth // inner
+    short = inner // quad
+    target_row = lax.broadcasted_iota(jnp.int32, (inner, inner), 0)
+    source_col = lax.broadcasted_iota(jnp.int32, (inner, inner), 1)
+    order = (source_col % quad) * short + source_col // quad == target_row
+    order = jnp.where(order, 1.0, 0.0).astype(jnp.bfloat16)
+    turned = lax.dot_general(
+        order, stacked, (((1,), (1,)), ((), ())), preferred_element_type=jnp.float32
+    ).astype(jnp.bfloat16)
+    real_part, imag_part = turned[:, :inner], turned[:, inner:]
+    left = jnp.concatenate(
+        [
+            jnp.concatenate([real_part, -imag_part], axis=1),
+            jnp.concatenate([imag_part, real_part], axis=1),
+        ],
+        axis=0,
+    )
+    for chunk in range(CHUNKS):
+        take_in(chunk)
+
+    for copy in last:
+        copy.wait()
+    arrived = jnp.concatenate([back[m] for m in range(peers)], axis=0)
+    right = jnp.concatenate(
+        [
+            jnp.concatenate(
+                [
+                    arrived[s * inner : (s + 1) * inner, comp * inner : (comp + 1) * inner]
+                    for s in range(slabs)
+                ],
+                axis=1,
+            )
+            for comp in range(2)
+        ],
+        axis=0,
+    )
+    final = dot(left, right).astype(jnp.bfloat16)
+    rows = jnp.concatenate(
+        [
+            jnp.concatenate(
+                [
+                    final[
+                        comp * inner + q * short : comp * inner + (q + 1) * short,
+                        s * inner : (s + 1) * inner,
+                    ]
+                    for q in range(quad)
+                ],
+                axis=1,
+            )
+            for comp in range(2)
+            for s in range(slabs)
+        ],
+        axis=0,
+    )
+    count = slabs * short
+    named = groups_ref[...]
+    real_sum = jnp.zeros(out_ref.shape[1:], jnp.float32)
+    imag_sum = jnp.zeros(out_ref.shape[1:], jnp.float32)
+
+    def project(group, real_sum, imag_sum):
+        by_real = dot(rows, weights[group, 0])
+        by_imag = dot(rows, weights[group, 1])
+        here = named == group
+        real_sum = jnp.where(here, by_real[:count] - by_imag[count:], real_sum)
+        imag_sum = jnp.where(here, by_imag[:count] + by_real[count:], imag_sum)
+        return real_sum, imag_sum
+
+    load_proj.wait()
+    real_sum, imag_sum = project(home, real_sum, imag_sum)
+    own.wait()
+    real_sum, imag_sum = project(sibling, real_sum, imag_sum)
+    real_sum, imag_sum = project(across, real_sum, imag_sum)
+    for copy in over_core:
+        copy.wait()
+    real_sum, imag_sum = project(across_sibling, real_sum, imag_sum)
+    for gain in [jnp.minimum(g, 1.0) for g in gains] + [jnp.maximum(g, 1.0) for g in gains]:
+        real_sum = real_sum * gain
+        imag_sum = imag_sum * gain
+    out_ref[0] = real_sum.astype(jnp.bfloat16)
+    out_ref[1] = imag_sum.astype(jnp.bfloat16)
+    for copy in over_x:
+        copy.wait_send()
+    for copy in over_y:
+        copy.wait_send()
+
+
+def local(stem_state, branch_mats, branch_modes, out_proj, groups):
+    slabs, inner = stem_state.shape[3], stem_state.shape[4]
+    legs, branches = branch_mats.shape[:2]
+    depth, out_len = out_proj.shape[2:]
+    peers = lax.axis_size("modes")
+    rows = slabs * inner
+    row_total = rows * inner // depth
+    part = rows // peers
+    bf16 = jnp.bfloat16
+    whole = pl.BlockSpec(memory_space=pl.ANY)
+    result = pl.pallas_call(
+        functools.partial(fused, (peers, legs, branches, slabs, inner, depth)),
+        out_shape=jax.ShapeDtypeStruct((2, row_total, out_len), bf16),
+        in_specs=[
+            whole,
+            whole,
+            pl.BlockSpec(memory_space=pltpu.SMEM),
+            whole,
+            pl.BlockSpec(memory_space=pltpu.VMEM),
+        ],
+        out_specs=pl.BlockSpec(memory_space=pltpu.VMEM),
+        scratch_shapes=[
+            pltpu.VMEM(branch_mats.shape, bf16),
+            pltpu.VMEM((peers, 2, part, inner), bf16),
+            pltpu.VMEM((peers, part, 2 * inner), bf16),
+            pltpu.VMEM((peers, part, 2 * inner), bf16),
+            pltpu.VMEM((lax.axis_size("half"), 2, depth, out_len), bf16),
+            pltpu.SemaphoreType.DMA((3,)),
+            pltpu.SemaphoreType.DMA((peers - 1,)),
+            pltpu.SemaphoreType.DMA((peers - 1,)),
+            pltpu.SemaphoreType.DMA((peers - 1,)),
+            pltpu.SemaphoreType.DMA((peers - 1,)),
+            pltpu.SemaphoreType.DMA((CHUNKS,)),
+            pltpu.SemaphoreType.DMA((CHUNKS,)),
+            pltpu.SemaphoreType.DMA((CHUNKS,)),
+            pltpu.SemaphoreType.DMA((CHUNKS,)),
+            pltpu.SemaphoreType.DMA((1 + 2 * CHUNKS,)),
+            pltpu.SemaphoreType.DMA((1 + 2 * CHUNKS,)),
+        ],
+        compiler_params=pltpu.CompilerParams(
+            collective_id=0, has_side_effects=True, vmem_limit_bytes=40 * 1024 * 1024
+        ),
+    )(
+        stem_state.reshape(2, rows, inner),
+        branch_mats,
+        branch_modes,
+        out_proj.reshape(out_proj.shape[1:]),
+        groups.reshape(row_total, 1),
+    )
+    return result.reshape(1, 1, 2, row_total, out_len)
+
+
 def solution(mesh):
     placed = (
         P(None, ("slices", "modes"), "half", None, None, None),
@@ -65,8 +426,10 @@
         P("half", None, None, None),
         P(("slices", "modes"), "half", None, None),
     )
+    sizes = dict(mesh.shape)
+    in_kernel = sizes["half"] == 4 and sizes["slices"] == 2 and sizes["modes"] <= 4
     return jax.shard_map(
-        local,
+        local if in_kernel else stepwise,
         mesh=mesh,
         in_specs=placed,
         out_specs=P(("slices", "modes"), "half", None, None, None),

time: 111 us -> 24.8 us (0.22)
  waiting for transfers between devices: 23.7 us -> 0 us
  Pallas kernels: 0 us -> 19.2 us
  loops' own time: 17.5 us -> 0 us
  other arithmetic: 17 us -> 0 us
  starting transfers between devices: 16.3 us -> 0 us
  between operations: 13.6 us -> 0.01 us
  local copies, waits for them, and re-layouts: 16.3 us -> 5.41 us
  matrix products: 6.35 us -> 0 us
    all_to_all x4 -> x0, waiting for transfers between devices: 23 us -> none  [local(): lax.all_to_all(pieces, 'modes', split_axis=0, concat_axis=0, tiled=True)]
    pallas_call x0 -> x1, Pallas kernels: none -> 19.2 us  [local(): pl.pallas_call(functools.partial(fused, (peers, legs, branches, slabs, in...]
    another operation x28 -> x0, loops' own time: 17.5 us -> none  [the longest x4 16.8 us: local(): state = lax.fori_loop(0, branch_total, advance, state)]
    all_to_all x4 -> x0, starting transfers between devices: 16.3 us -> none  [local(): lax.all_to_all(pieces, 'modes', split_axis=0, concat_axis=0, tiled=True)]
    eq x25 -> x0, other arithmetic: 15.4 us -> none  [the longest x24 15.4 us: advance(): branch_modes[leg][branch] == 0]
    dot_general x25 -> x0, matrix products: 6.35 us -> none  [the longest x12 2.63 us: contract_first(): jnp.einsum('isbc,ijbd->jsdc', state, wide, preferred_element_type=jnp.flo...]
    reshape x12 -> x1, local copies, waits for them, and re-layouts: 6.83 us -> 0.74 us  [local(): groups.reshape(row_total, 1)]
    unnamed x7 -> x9, local copies, waits for them, and re-layouts: 1.43 us -> 4.67 us
  transfers between devices with their start and end apart: 5 -> 0, of which waited for: 4 -> 0; matrix products, arithmetic and copies ran while one was open for 8% -> 0% of each run, Pallas kernels for 0% -> 0%
where the time goes in v1:
time: 24.8 us; the launch traced here: 24.6 us
  Pallas kernels  19.2 us (77%)
  local copies, waits for them, and re-layouts  5.41 us (22%)
    pallas_call x1, Pallas kernels, local(): pl.pallas_call(functools.partial(fused, (peers, legs, branches, slabs, in...  19.2 us
    unnamed x9, local copies, waits for them, and re-layouts  4.67 us
    reshape x1, local copies, waits for them, and re-layouts, local(): groups.reshape(row_total, 1)  0.74 us

profile of v1, /device:TPU:0, one launch (start us, length us, event | category | flops | bytes accessed | tf_op | source)
XLA Modules:
  0.0 24.6 jit_solution(16279326462652234608)
XLA Ops:
  0.0 0.7 %copy.6.groups_ref = s32[64,1]{1,0:T(8,128)S(1)} copy(s32[64,1]{0,1:T(1,128)} %bitcast.7) | data formatting | bytes 512 | tf_op jit(solution)/shard_map/reshape | solution.py:416
  0.7 0.0 copy-start
  0.7 1.4 %copy-done = bf16[4,6,2,128,128]{4,3,2,1,0:T(8,128)(2,1)S(1)} copy-done((bf16[4,6,2,128,128]{4,3,2,1,0:T(8,128)(2,1)S(1)}, bf16[4,6,2,128,128]{4,3,2,1,0:T(8,128)(2,1)}, u32[]{:S(2)}) %copy-start) | copy-done | bytes 1572888
  2.2 0.0 copy-start.1
  2.2 1.0 %copy-done.1 = bf16[1,2,512,256]{3,2,1,0:T(8,128)(2,1)S(1)} copy-done((bf16[1,2,512,256]{3,2,1,0:T(8,128)(2,1)S(1)}, bf16[1,2,512,256]{3,2,1,0:T(8,128)(2,1)}, u32[]{:S(2)}) %copy-start.1) | copy-done | bytes 524312
  3.2 0.0 copy-start.2
  3.2 0.9 %copy-done.2 = bf16[2,1,1,2,128,128]{5,4,3,2,1,0:T(8,128)(2,1)S(1)} copy-done((bf16[2,1,1,2,128,128]{5,4,3,2,1,0:T(8,128)(2,1)S(1)}, bf16[2,1,1,2,128,128]{5,4,3,2,1,0:T(8,128)(2,1)}, u32[]{:S(2)}) %copy-start.2) | copy-done | bytes 131096
  4.1 0.0 copy-start.3
  4.1 0.7 %copy-done.3 = s32[4,6]{1,0:T(4,128)S(1)} copy-done((s32[4,6]{1,0:T(4,128)S(1)}, s32[4,6]{1,0:T(4,128)}, u32[]{:S(2)}) %copy-start.3) | copy-done | bytes 120
  4.8 19.2 %shard_map.55 = bf16[2,64,256]{2,1,0:T(8,128)(2,1)S(1)} custom-call(bf16[2,256,128]{2,1,0:T(8,128)(2,1)S(1)} %bitcast.6, bf16[4,6,2,128,128]{4,3,2,1,0:T(8,128)(2,1)S(1)} %copy-done, s32[4,6]{1,0:T(4,128)S(1)} %copy-done.3, bf16[2,512,256]{2,1,0:T(8,128)(2,1)S(1)} %bitcast.4, s32[64,1]{1,0:T(8,128)S(1)} %copy.6.groups_ref), custom_call_target="tpu_custom_call" | custom-call | tf_op jit(solution)/shard_map/pallas_call | solution.py:379
  24.0 0.6 %copy.8 = bf16[1,1,2,64,256]{4,3,2,1,0:T(8,128)(2,1)} copy(bf16[1,1,2,64,256]{4,3,2,1,0:T(8,128)(2,1)S(1)} %bitcast.5) | data formatting | bytes 131072
Async XLA Ops:
  0.7 1.4 %copy-start = (bf16[4,6,2,128,128]{4,3,2,1,0:T(8,128)(2,1)S(1)}, bf16[4,6,2,128,128]{4,3,2,1,0:T(8,128)(2,1)}, u32[]{:S(2)}) copy-start(bf16[4,6,2,128,128]{4,3,2,1,0:T(8,128)(2,1)} %mats_hbm.1) | copy-start | bytes 4718596
  2.2 1.0 %copy-start.1 = (bf16[1,2,512,256]{3,2,1,0:T(8,128)(2,1)S(1)}, bf16[1,2,512,256]{3,2,1,0:T(8,128)(2,1)}, u32[]{:S(2)}) copy-start(bf16[1,2,512,256]{3,2,1,0:T(8,128)(2,1)} %param.8) | copy-start | bytes 1572868
  3.2 0.9 %copy-start.2 = (bf16[2,1,1,2,128,128]{5,4,3,2,1,0:T(8,128)(2,1)S(1)}, bf16[2,1,1,2,128,128]{5,4,3,2,1,0:T(8,128)(2,1)}, u32[]{:S(2)}) copy-start(bf16[2,1,1,2,128,128]{5,4,3,2,1,0:T(8,128)(2,1)} %param.5) | copy-start | bytes 393220
  4.1 0.7 %copy-start.3 = (s32[4,6]{1,0:T(4,128)S(1)}, s32[4,6]{1,0:T(4,128)}, u32[]{:S(2)}) copy-start(s32[4,6]{1,0:T(4,128)} %modes_ref.1) | copy-start | bytes 292

commit v2 on v1

--- a/solution.py
+++ b/solution.py
@@ -82,10 +82,12 @@
     sizes,
     state_ref,
     mats_hbm,
+    modes_hbm,
+    proj_ref,
+    groups_hbm,
+    out_ref,
     modes_ref,
-    proj_ref,
     groups_ref,
-    out_ref,
     mats,
     got,
     leave,
@@ -117,6 +119,8 @@
     half_depth = depth // 2
     piece = half_depth // CHUNKS
 
+    load_modes = pltpu.make_async_copy(modes_hbm, modes_ref, local_sem.at[3])
+    load_modes.start()
     load_mats = pltpu.make_async_copy(mats_hbm, mats, local_sem.at[0])
     load_mats.start()
     load_own = pltpu.make_async_copy(
@@ -125,6 +129,8 @@
     load_own.start()
     load_proj = pltpu.make_async_copy(proj_ref, weights.at[home], local_sem.at[2])
     load_proj.start()
+    load_groups = pltpu.make_async_copy(groups_hbm, groups_ref, local_sem.at[4])
+    load_groups.start()
 
     barrier = pltpu.get_barrier_semaphore()
     for step in range(1, peers):
@@ -205,6 +211,7 @@
         over_y[chunk].wait_recv()
         to_core(other_row, chunk, 1 + CHUNKS + chunk)
 
+    load_modes.wait()
     load_mats.wait()
     lanes = lax.broadcasted_iota(jnp.int32, (inner, 2 * inner), 1)
     sublanes = lax.broadcasted_iota(jnp.int32, (inner, 2 * inner), 0)
@@ -223,6 +230,7 @@
             value = dot(chosen, wide_of(top))
             over_b[leg] = jnp.where(is_b, value, over_b[leg])
             over_c[leg] = jnp.where(is_b, over_c[leg], value)
+    hand_on(0)
     gains = []
     wides = []
     for leg in range(legs):
@@ -233,6 +241,7 @@
         gains.append(gain)
         over_b[leg] = scaled.astype(jnp.bfloat16)
 
+    hand_on(1)
     load_own.wait()
     for copy in first:
         copy.wait()
@@ -256,6 +265,9 @@
                 both.append(taken)
             swapped.append(jnp.concatenate(both, axis=1))
         values = jnp.concatenate(swapped, axis=0).astype(jnp.bfloat16)
+        if leg == 1:
+            hand_on(2)
+            take_in(0)
     for m in range(peers):
         leave[m] = values[m * part : (m + 1) * part]
 
@@ -273,8 +285,8 @@
         copy.start()
         last.append(copy)
     back[me] = leave[me]
-    for chunk in range(CHUNKS):
-        hand_on(chunk)
+    hand_on(3)
+    take_in(1)
 
     total = over_b[0]
     for leg in range(1, legs):
@@ -297,8 +309,8 @@
         ],
         axis=0,
     )
-    for chunk in range(CHUNKS):
-        take_in(chunk)
+    take_in(2)
+    take_in(3)
 
     for copy in last:
         copy.wait()
@@ -335,14 +347,18 @@
         axis=0,
     )
     count = slabs * short
-    named = groups_ref[...]
+    load_groups.wait()
+    spread = jnp.broadcast_to(groups_ref[...].astype(jnp.float32), (count, count))
+    on_diagonal = lax.broadcasted_iota(jnp.int32, (count, count), 0)
+    on_diagonal = on_diagonal == lax.broadcasted_iota(jnp.int32, (count, count), 1)
+    named = jnp.sum(jnp.where(on_diagonal, spread, 0.0), axis=1, keepdims=True)
     real_sum = jnp.zeros(out_ref.shape[1:], jnp.float32)
     imag_sum = jnp.zeros(out_ref.shape[1:], jnp.float32)
 
     def project(group, real_sum, imag_sum):
         by_real = dot(rows, weights[group, 0])
         by_imag = dot(rows, weights[group, 1])
-        here = named == group
+        here = named == group.astype(jnp.float32)
         real_sum = jnp.where(here, by_real[:count] - by_imag[count:], real_sum)
         imag_sum = jnp.where(here, by_imag[:count] + by_real[count:], imag_sum)
         return real_sum, imag_sum
@@ -382,18 +398,20 @@
         in_specs=[
             whole,
             whole,
-            pl.BlockSpec(memory_space=pltpu.SMEM),
             whole,
-            pl.BlockSpec(memory_space=pltpu.VMEM),
+            whole,
+            whole,
         ],
         out_specs=pl.BlockSpec(memory_space=pltpu.VMEM),
         scratch_shapes=[
+            pltpu.SMEM(branch_modes.shape, jnp.int32),
+            pltpu.VMEM((1, row_total), jnp.int32),
             pltpu.VMEM(branch_mats.shape, bf16),
             pltpu.VMEM((peers, 2, part, inner), bf16),
             pltpu.VMEM((peers, part, 2 * inner), bf16),
             pltpu.VMEM((peers, part, 2 * inner), bf16),
             pltpu.VMEM((lax.axis_size("half"), 2, depth, out_len), bf16),
-            pltpu.SemaphoreType.DMA((3,)),
+            pltpu.SemaphoreType.DMA((5,)),
             pltpu.SemaphoreType.DMA((peers - 1,)),
             pltpu.SemaphoreType.DMA((peers - 1,)),
             pltpu.SemaphoreType.DMA((peers - 1,)),
@@ -406,14 +424,14 @@
             pltpu.SemaphoreType.DMA((1 + 2 * CHUNKS,)),
         ],
         compiler_params=pltpu.CompilerParams(
-            collective_id=0, has_side_effects=True, vmem_limit_bytes=40 * 1024 * 1024
+            collective_id=0, has_side_effects=True, vmem_limit_bytes=60 * 1024 * 1024
         ),
     )(
         stem_state.reshape(2, rows, inner),
         branch_mats,
         branch_modes,
         out_proj.reshape(out_proj.shape[1:]),
-        groups.reshape(row_total, 1),
+        groups.reshape(1, row_total),
     )
     return result.reshape(1, 1, 2, row_total, out_len)
 

time: 24.8 us -> 21.4 us (0.86)
  local copies, waits for them, and re-layouts: 5.41 us -> 1.47 us
  Pallas kernels: 19.2 us -> 19.8 us
    unnamed x9 -> x1, local copies, waits for them, and re-layouts: 4.67 us -> 1.47 us
    reshape x1 -> x0, local copies, waits for them, and re-layouts: 0.74 us -> none  [local(): groups.reshape(row_total, 1)]
    pallas_call x1, Pallas kernels: 19.2 us -> 19.8 us  [local(): pl.pallas_call(functools.partial(fused, (peers, legs, branches, slabs, in...]
where the time goes in v2:
time: 21.4 us; the launch traced here: 21.3 us
  Pallas kernels  19.8 us (93%)
  local copies, waits for them, and re-layouts  1.47 us (7%)
    pallas_call x1, Pallas kernels, local(): pl.pallas_call(functools.partial(fused, (peers, legs, branches, slabs, in...  19.8 us
    unnamed x1, local copies, waits for them, and re-layouts  1.47 us

profile of v2, /device:TPU:0, one launch (start us, length us, event | category | flops | bytes accessed | tf_op | source)
XLA Modules:
  0.0 21.3 jit_solution(16274996126595361981)
XLA Ops:
  0.0 19.8 %shard_map.55 = bf16[2,64,256]{2,1,0:T(8,128)(2,1)} custom-call(bf16[2,256,128]{2,1,0:T(8,128)(2,1)} %bitcast.6, bf16[4,6,2,128,128]{4,3,2,1,0:T(8,128)(2,1)} %mats_hbm.1, s32[4,6]{1,0:T(4,128)} %modes_hbm.1, bf16[2,512,256]{2,1,0:T(8,128)(2,1)} %bitcast.4, s32[1,64]{1,0:T(1,128)} %bitcast.7), custom_call_target="tpu_custom_call" | custom-call | tf_op jit(solution)/shard_map/pallas_call | solution.py:395
  19.8 1.5 %copy.7 = bf16[1,1,2,64,256]{4,3,2,1,0:T(8,128)(2,1)} copy(bf16[1,1,2,64,256]{4,3,2,1,0:T(8,128)(2,1)} %bitcast.5) | data formatting | bytes 131072

commit v3 on v2

--- a/solution.py
+++ b/solution.py
@@ -75,7 +75,7 @@
 def normal(top):
     largest = jnp.max(jnp.abs(top), axis=(0, 1), keepdims=True)
     largest = jnp.where(largest > 0.0, largest, 1.0)
-    return top / largest, largest
+    return top * (1.0 / largest), largest
 
 
 def fused(
@@ -89,6 +89,7 @@
     modes_ref,
     groups_ref,
     mats,
+    past,
     got,
     leave,
     back,
@@ -215,42 +216,29 @@
     load_mats.wait()
     lanes = lax.broadcasted_iota(jnp.int32, (inner, 2 * inner), 1)
     sublanes = lax.broadcasted_iota(jnp.int32, (inner, 2 * inner), 0)
-    identity = jnp.where(lanes == sublanes, 1.0, 0.0).astype(jnp.float32)
-    over_b, over_c = [], []
-    for leg in range(legs):
-        top = jnp.concatenate([mats[leg, 0, 0], mats[leg, 0, 1]], axis=1).astype(jnp.float32)
+    identity = jnp.where(lanes == sublanes, 1.0, 0.0).astype(jnp.bfloat16)
+    last_b, last_c = {}, {}
+
+    def start_leg(leg):
+        past[leg, 0] = identity
+        past[leg, 1, :, :inner] = mats[leg, 0, 0]
+        past[leg, 1, :, inner:] = mats[leg, 0, 1]
         is_b = modes_ref[leg, 0] == 0
-        over_b.append(jnp.where(is_b, top, identity))
-        over_c.append(jnp.where(is_b, identity, top))
-    for branch in range(1, branches):
-        for leg in range(legs):
-            is_b = modes_ref[leg, branch] == 0
-            top = jnp.concatenate([mats[leg, branch, 0], mats[leg, branch, 1]], axis=1)
-            chosen = jnp.where(is_b, over_b[leg], over_c[leg]).astype(jnp.bfloat16)
-            value = dot(chosen, wide_of(top))
-            over_b[leg] = jnp.where(is_b, value, over_b[leg])
-            over_c[leg] = jnp.where(is_b, over_c[leg], value)
-    hand_on(0)
-    gains = []
-    wides = []
-    for leg in range(legs):
-        scaled, gain = normal(over_c[leg])
-        gains.append(gain)
-        wides.append(wide_of(scaled.astype(jnp.bfloat16)))
-        scaled, gain = normal(over_b[leg])
-        gains.append(gain)
-        over_b[leg] = scaled.astype(jnp.bfloat16)
-
-    hand_on(1)
-    load_own.wait()
-    for copy in first:
-        copy.wait()
-    values = jnp.concatenate(
-        [jnp.concatenate([got[m, 0], got[m, 1]], axis=1) for m in range(peers)], axis=0
-    )
+        last_b[leg] = jnp.where(is_b, 1, 0)
+        last_c[leg] = jnp.where(is_b, 0, 1)
+
+    def next_branch(leg, branch):
+        is_b = modes_ref[leg, branch] == 0
+        top = jnp.concatenate([mats[leg, branch, 0], mats[leg, branch, 1]], axis=1)
+        before = past[leg, jnp.where(is_b, last_b[leg], last_c[leg])]
+        past[leg, branch + 1] = dot(before, wide_of(top)).astype(jnp.bfloat16)
+        last_b[leg] = jnp.where(is_b, branch + 1, last_b[leg])
+        last_c[leg] = jnp.where(is_b, last_c[leg], branch + 1)
+
     block = lax.broadcasted_iota(jnp.int32, (part, inner), 1) // width
-    for leg in range(legs):
-        product = dot(values, wides[leg])
+
+    def apply_leg(values, wide):
+        product = dot(values, wide)
         swapped = []
         for m in range(peers):
             both = []
@@ -264,10 +252,39 @@
                     taken = tile if taken is None else jnp.where(block == t, tile, taken)
                 both.append(taken)
             swapped.append(jnp.concatenate(both, axis=1))
-        values = jnp.concatenate(swapped, axis=0).astype(jnp.bfloat16)
-        if leg == 1:
-            hand_on(2)
-            take_in(0)
+        return jnp.concatenate(swapped, axis=0).astype(jnp.bfloat16)
+
+    gains = []
+
+    def scaled(top):
+        top, gain = normal(top.astype(jnp.float32))
+        gains.append(gain)
+        return top.astype(jnp.bfloat16)
+
+    early = min(2, legs)
+    for leg in range(early):
+        start_leg(leg)
+    for branch in range(1, branches):
+        for leg in range(early):
+            next_branch(leg, branch)
+    load_own.wait()
+    for copy in first:
+        copy.wait()
+    hand_on(0)
+    values = jnp.concatenate(
+        [jnp.concatenate([got[m, 0], got[m, 1]], axis=1) for m in range(peers)], axis=0
+    )
+    for leg in range(early):
+        values = apply_leg(values, wide_of(past[leg, last_c[leg]]))
+    for leg in range(early, legs):
+        start_leg(leg)
+    for branch in range(1, branches):
+        for leg in range(early, legs):
+            next_branch(leg, branch)
+    hand_on(1)
+    hand_on(2)
+    for leg in range(early, legs):
+        values = apply_leg(values, wide_of(scaled(past[leg, last_c[leg]])))
     for m in range(peers):
         leave[m] = values[m * part : (m + 1) * part]
 
@@ -286,11 +303,15 @@
         last.append(copy)
     back[me] = leave[me]
     hand_on(3)
-    take_in(1)
-
-    total = over_b[0]
-    for leg in range(1, legs):
-        total = dot(total, wide_of(over_b[leg])).astype(jnp.bfloat16)
+    take_in(0)
+
+    factors = [past[leg, last_b[leg]] for leg in range(legs)]
+    while len(factors) > 1:
+        pairs = [
+            scaled(dot(factors[i], wide_of(factors[i + 1]))) for i in range(0, len(factors) - 1, 2)
+        ]
+        factors = pairs + factors[len(pairs) * 2 :]
+    total = factors[0]
     stacked = jnp.concatenate([total[:, :inner], total[:, inner:]], axis=0)
     quad = depth // inner
     short = inner // quad
@@ -309,6 +330,7 @@
         ],
         axis=0,
     )
+    take_in(1)
     take_in(2)
     take_in(3)
 
@@ -374,8 +396,8 @@
     for gain in [jnp.minimum(g, 1.0) for g in gains] + [jnp.maximum(g, 1.0) for g in gains]:
         real_sum = real_sum * gain
         imag_sum = imag_sum * gain
-    out_ref[0] = real_sum.astype(jnp.bfloat16)
-    out_ref[1] = imag_sum.astype(jnp.bfloat16)
+    out_ref[0] = real_sum
+    out_ref[1] = imag_sum
     for copy in over_x:
         copy.wait_send()
     for copy in over_y:
@@ -394,7 +416,7 @@
     whole = pl.BlockSpec(memory_space=pl.ANY)
     result = pl.pallas_call(
         functools.partial(fused, (peers, legs, branches, slabs, inner, depth)),
-        out_shape=jax.ShapeDtypeStruct((2, row_total, out_len), bf16),
+        out_shape=jax.ShapeDtypeStruct((2, row_total, out_len), jnp.float32),
         in_specs=[
             whole,
             whole,
@@ -407,6 +429,7 @@
             pltpu.SMEM(branch_modes.shape, jnp.int32),
             pltpu.VMEM((1, row_total), jnp.int32),
             pltpu.VMEM(branch_mats.shape, bf16),
+            pltpu.VMEM((legs, branches + 1, inner, 2 * inner), bf16),
             pltpu.VMEM((peers, 2, part, inner), bf16),
             pltpu.VMEM((peers, part, 2 * inner), bf16),
             pltpu.VMEM((peers, part, 2 * inner), bf16),
@@ -433,7 +456,7 @@
         out_proj.reshape(out_proj.shape[1:]),
         groups.reshape(1, row_total),
     )
-    return result.reshape(1, 1, 2, row_total, out_len)
+    return result.astype(bf16).reshape(1, 1, 2, row_total, out_len)
 
 
 def solution(mesh):

time: 21.4 us -> 20.9 us (0.977)
  other arithmetic: 0 us -> 1.54 us
  local copies, waits for them, and re-layouts: 1.47 us -> 0 us
  Pallas kernels: 19.8 us -> 19.2 us
    reshape x0 -> x1, other arithmetic: none -> 1.54 us  [local(): return result.astype(bf16).reshape(1, 1, 2, row_total, out_len)]
    unnamed x1 -> x0, local copies, waits for them, and re-layouts: 1.47 us -> none
    pallas_call x1, Pallas kernels: 19.8 us -> 19.2 us  [local(): pl.pallas_call(functools.partial(fused, (peers, legs, branches, slabs, in...]
where the time goes in v3:
time: 20.9 us; the launch traced here: 20.8 us
  Pallas kernels  19.2 us (92%)
  other arithmetic  1.54 us (7%)
    pallas_call x1, Pallas kernels, local(): pl.pallas_call(functools.partial(fused, (peers, legs, branches, slabs, in...  19.2 us
    reshape x1, other arithmetic, local(): return result.astype(bf16).reshape(1, 1, 2, row_total, out_len)  1.54 us

profile of v3, /device:TPU:0, one launch (start us, length us, event | category | flops | bytes accessed | tf_op | source)
XLA Modules:
  0.0 20.8 jit_solution(16362541954648039854)
XLA Ops:
  0.0 19.2 %shard_map.55 = f32[2,64,256]{2,1,0:T(8,128)} custom-call(bf16[2,256,128]{2,1,0:T(8,128)(2,1)} %bitcast.6, bf16[4,6,2,128,128]{4,3,2,1,0:T(8,128)(2,1)} %mats_hbm.1, s32[4,6]{1,0:T(4,128)} %modes_hbm.1, bf16[2,512,256]{2,1,0:T(8,128)(2,1)} %bitcast.5, s32[1,64]{1,0:T(1,128)} %bitcast.7), custom_call_target="tpu_custom_call" | custom-call | tf_op jit(solution)/shard_map/pallas_call | solution.py:417
  19.2 1.5 %convert_bitcast_fusion = bf16[1,1,2,64,256]{4,3,2,1,0:T(8,128)(2,1)} fusion(f32[2,64,256]{2,1,0:T(8,128)} %shard_map.55), kind=kLoop, calls=%fused_computation | loop fusion | flops 32768 | bytes 196608 | tf_op jit(solution)/shard_map/reshape | solution.py:459

commit v4 on v3

--- a/solution.py
+++ b/solution.py
@@ -8,7 +8,8 @@
 from jax.sharding import PartitionSpec as P
 
 MESH = pl.DeviceIdType.MESH
-CHUNKS = 4
+CHUNKS = 8
+DIRECT = 5
 
 
 def widen(matrix):
@@ -117,21 +118,8 @@
     across_sibling = lax.rem(sibling + 2, 4)
     other_row = 1 - row
     part = got.shape[2]
-    half_depth = depth // 2
-    piece = half_depth // CHUNKS
-
-    load_modes = pltpu.make_async_copy(modes_hbm, modes_ref, local_sem.at[3])
-    load_modes.start()
-    load_mats = pltpu.make_async_copy(mats_hbm, mats, local_sem.at[0])
-    load_mats.start()
-    load_own = pltpu.make_async_copy(
-        state_ref.at[:, pl.ds(me * part, part), :], got.at[me], local_sem.at[1]
-    )
-    load_own.start()
-    load_proj = pltpu.make_async_copy(proj_ref, weights.at[home], local_sem.at[2])
-    load_proj.start()
-    load_groups = pltpu.make_async_copy(groups_hbm, groups_ref, local_sem.at[4])
-    load_groups.start()
+    piece = depth // CHUNKS
+    handed = CHUNKS - DIRECT
 
     barrier = pltpu.get_barrier_semaphore()
     for step in range(1, peers):
@@ -141,6 +129,19 @@
     pl.semaphore_signal(barrier, inc=1, device_id={"half": sibling}, device_id_type=MESH)
     pl.semaphore_signal(barrier, inc=1, device_id={"half": across}, device_id_type=MESH)
     pl.semaphore_signal(barrier, inc=1, device_id={"slices": other_row}, device_id_type=MESH)
+
+    load_modes = pltpu.make_async_copy(modes_hbm, modes_ref, local_sem.at[0])
+    load_modes.start()
+    load_mats = []
+    for leg in range(legs):
+        load_mats.append(
+            pltpu.make_async_copy(mats_hbm.at[leg], mats.at[leg], local_sem.at[4 + leg])
+        )
+        load_mats[leg].start()
+    load_own = pltpu.make_async_copy(
+        state_ref.at[:, pl.ds(me * part, part), :], got.at[me], local_sem.at[1]
+    )
+    load_own.start()
     pl.semaphore_wait(barrier, peers + 2)
 
     first = []
@@ -158,10 +159,11 @@
         first.append(copy)
 
     def rows_of(which, chunk):
-        return pl.ds(which * half_depth + chunk * piece, piece)
+        forward = pl.multiple_of(which * (CHUNKS - 1) * piece + (1 - 2 * which) * chunk * piece, piece)
+        return pl.ds(forward, piece)
 
     over_x, over_y, over_core = [], [], []
-    for chunk in range(CHUNKS):
+    for chunk in range(DIRECT):
         copy = pltpu.make_async_remote_copy(
             src_ref=proj_ref.at[:, rows_of(row, chunk), :],
             dst_ref=weights.at[home, :, rows_of(row, chunk), :],
@@ -180,7 +182,8 @@
         device_id={"half": sibling},
         device_id_type=MESH,
     )
-    own.start()
+    load_proj = pltpu.make_async_copy(proj_ref, weights.at[home], local_sem.at[2])
+    load_groups = pltpu.make_async_copy(groups_hbm, groups_ref, local_sem.at[3])
 
     def to_core(which, chunk, number):
         copy = pltpu.make_async_remote_copy(
@@ -194,32 +197,33 @@
         copy.start()
         over_core.append(copy)
 
-    def hand_on(chunk):
+    def from_x(chunk):
         over_x[chunk].wait_recv()
-        copy = pltpu.make_async_remote_copy(
-            src_ref=weights.at[across, :, rows_of(row, chunk), :],
-            dst_ref=weights.at[across, :, rows_of(row, chunk), :],
-            send_sem=y_send.at[chunk],
-            recv_sem=y_recv.at[chunk],
-            device_id={"slices": other_row},
-            device_id_type=MESH,
-        )
-        copy.start()
-        over_y.append(copy)
+        if chunk < handed:
+            copy = pltpu.make_async_remote_copy(
+                src_ref=weights.at[across, :, rows_of(row, chunk), :],
+                dst_ref=weights.at[across, :, rows_of(row, chunk), :],
+                send_sem=y_send.at[chunk],
+                recv_sem=y_recv.at[chunk],
+                device_id={"slices": other_row},
+                device_id_type=MESH,
+            )
+            copy.start()
+            over_y.append(copy)
         to_core(row, chunk, 1 + chunk)
 
-    def take_in(chunk):
+    def from_y(chunk):
         over_y[chunk].wait_recv()
-        to_core(other_row, chunk, 1 + CHUNKS + chunk)
+        to_core(other_row, chunk, 1 + DIRECT + chunk)
 
     load_modes.wait()
-    load_mats.wait()
     lanes = lax.broadcasted_iota(jnp.int32, (inner, 2 * inner), 1)
     sublanes = lax.broadcasted_iota(jnp.int32, (inner, 2 * inner), 0)
     identity = jnp.where(lanes == sublanes, 1.0, 0.0).astype(jnp.bfloat16)
     last_b, last_c = {}, {}
 
     def start_leg(leg):
+        load_mats[leg].wait()
         past[leg, 0] = identity
         past[leg, 1, :, :inner] = mats[leg, 0, 0]
         past[leg, 1, :, inner:] = mats[leg, 0, 1]
@@ -262,29 +266,33 @@
         return top.astype(jnp.bfloat16)
 
     early = min(2, legs)
-    for leg in range(early):
-        start_leg(leg)
-    for branch in range(1, branches):
-        for leg in range(early):
-            next_branch(leg, branch)
+    for group in (range(early), range(early, legs)):
+        for leg in group:
+            start_leg(leg)
+        for branch in range(1, branches):
+            for leg in group:
+                next_branch(leg, branch)
+        if group[0] == 0:
+            own.start()
+            load_proj.start()
+            load_groups.start()
+    wides = []
+    for leg in range(legs):
+        top = past[leg, last_c[leg]]
+        wides.append(wide_of(top if leg < early else scaled(top)))
+    from_x(0)
     load_own.wait()
     for copy in first:
         copy.wait()
-    hand_on(0)
     values = jnp.concatenate(
         [jnp.concatenate([got[m, 0], got[m, 1]], axis=1) for m in range(peers)], axis=0
     )
-    for leg in range(early):
-        values = apply_leg(values, wide_of(past[leg, last_c[leg]]))
-    for leg in range(early, legs):
-        start_leg(leg)
-    for branch in range(1, branches):
-        for leg in range(early, legs):
-            next_branch(leg, branch)
-    hand_on(1)
-    hand_on(2)
-    for leg in range(early, legs):
-        values = apply_leg(values, wide_of(scaled(past[leg, last_c[leg]])))
+    values = apply_leg(values, wides[0])
+    from_x(1)
+    for leg in range(1, legs - 1):
+        values = apply_leg(values, wides[leg])
+    from_x(2)
+    values = apply_leg(values, wides[legs - 1])
     for m in range(peers):
         leave[m] = values[m * part : (m + 1) * part]
 
@@ -302,8 +310,6 @@
         copy.start()
         last.append(copy)
     back[me] = leave[me]
-    hand_on(3)
-    take_in(0)
 
     factors = [past[leg, last_b[leg]] for leg in range(legs)]
     while len(factors) > 1:
@@ -330,9 +336,11 @@
         ],
         axis=0,
     )
-    take_in(1)
-    take_in(2)
-    take_in(3)
+    from_y(0)
+    from_x(3)
+    from_y(1)
+    from_x(4)
+    from_y(2)
 
     for copy in last:
         copy.wait()
@@ -434,17 +442,17 @@
             pltpu.VMEM((peers, part, 2 * inner), bf16),
             pltpu.VMEM((peers, part, 2 * inner), bf16),
             pltpu.VMEM((lax.axis_size("half"), 2, depth, out_len), bf16),
-            pltpu.SemaphoreType.DMA((5,)),
+            pltpu.SemaphoreType.DMA((4 + legs,)),
             pltpu.SemaphoreType.DMA((peers - 1,)),
             pltpu.SemaphoreType.DMA((peers - 1,)),
             pltpu.SemaphoreType.DMA((peers - 1,)),
             pltpu.SemaphoreType.DMA((peers - 1,)),
-            pltpu.SemaphoreType.DMA((CHUNKS,)),
-            pltpu.SemaphoreType.DMA((CHUNKS,)),
-            pltpu.SemaphoreType.DMA((CHUNKS,)),
-            pltpu.SemaphoreType.DMA((CHUNKS,)),
-            pltpu.SemaphoreType.DMA((1 + 2 * CHUNKS,)),
-            pltpu.SemaphoreType.DMA((1 + 2 * CHUNKS,)),
+            pltpu.SemaphoreType.DMA((DIRECT,)),
+            pltpu.SemaphoreType.DMA((DIRECT,)),
+            pltpu.SemaphoreType.DMA((CHUNKS - DIRECT,)),
+            pltpu.SemaphoreType.DMA((CHUNKS - DIRECT,)),
+            pltpu.SemaphoreType.DMA((1 + CHUNKS,)),
+            pltpu.SemaphoreType.DMA((1 + CHUNKS,)),
         ],
         compiler_params=pltpu.CompilerParams(
             collective_id=0, has_side_effects=True, vmem_limit_bytes=60 * 1024 * 1024

time: 20.9 us -> 20.5 us (0.981)
  Pallas kernels: 19.2 us -> 18.8 us
    pallas_call x1, Pallas kernels: 19.2 us -> 18.8 us  [local(): pl.pallas_call(functools.partial(fused, (peers, legs, branches, slabs, in...]
where the time goes in v4:
time: 20.5 us; the launch traced here: 20.4 us
  Pallas kernels  18.8 us (92%)
  other arithmetic  1.54 us (8%)
    pallas_call x1, Pallas kernels, local(): pl.pallas_call(functools.partial(fused, (peers, legs, branches, slabs, in...  18.8 us
    reshape x1, other arithmetic, local(): return result.astype(bf16).reshape(1, 1, 2, row_total, out_len)  1.54 us

profile of v4, /device:TPU:0, one launch (start us, length us, event | category | flops | bytes accessed | tf_op | source)
XLA Modules:
  0.0 20.4 jit_solution(1642675284059721989)
XLA Ops:
  0.0 18.8 %shard_map.55 = f32[2,64,256]{2,1,0:T(8,128)} custom-call(bf16[2,256,128]{2,1,0:T(8,128)(2,1)} %bitcast.6, bf16[4,6,2,128,128]{4,3,2,1,0:T(8,128)(2,1)} %mats_hbm.1, s32[4,6]{1,0:T(4,128)} %modes_hbm.1, bf16[2,512,256]{2,1,0:T(8,128)(2,1)} %bitcast.5, s32[1,64]{1,0:T(1,128)} %bitcast.7), custom_call_target="tpu_custom_call" | custom-call | tf_op jit(solution)/shard_map/pallas_call | solution.py:425
  18.8 1.5 %convert_bitcast_fusion = bf16[1,1,2,64,256]{4,3,2,1,0:T(8,128)(2,1)} fusion(f32[2,64,256]{2,1,0:T(8,128)} %shard_map.55), kind=kLoop, calls=%fused_computation | loop fusion | flops 32768 | bytes 196608 | tf_op jit(solution)/shard_map/reshape | solution.py:467

commit v5 on v4

--- a/solution.py
+++ b/solution.py
@@ -10,6 +10,7 @@
 MESH = pl.DeviceIdType.MESH
 CHUNKS = 8
 DIRECT = 5
+WAVES = 2
 
 
 def widen(matrix):
@@ -144,19 +145,21 @@
     load_own.start()
     pl.semaphore_wait(barrier, peers + 2)
 
+    stripe = part // WAVES
     first = []
-    for step in range(1, peers):
-        target = lax.rem(me + step, peers)
-        copy = pltpu.make_async_remote_copy(
-            src_ref=state_ref.at[:, pl.ds(target * part, part), :],
-            dst_ref=got.at[me],
-            send_sem=first_send.at[step - 1],
-            recv_sem=first_recv.at[step - 1],
-            device_id={"modes": target},
-            device_id_type=MESH,
-        )
-        copy.start()
-        first.append(copy)
+    for wave in range(WAVES):
+        for step in range(1, peers):
+            target = lax.rem(me + step, peers)
+            copy = pltpu.make_async_remote_copy(
+                src_ref=state_ref.at[:, pl.ds(target * part + wave * stripe, stripe), :],
+                dst_ref=got.at[me, :, pl.ds(wave * stripe, stripe), :],
+                send_sem=first_send.at[wave, step - 1],
+                recv_sem=first_recv.at[wave, step - 1],
+                device_id={"modes": target},
+                device_id_type=MESH,
+            )
+            copy.start()
+            first.append(copy)
 
     def rows_of(which, chunk):
         forward = pl.multiple_of(which * (CHUNKS - 1) * piece + (1 - 2 * which) * chunk * piece, piece)
@@ -239,7 +242,7 @@
         last_b[leg] = jnp.where(is_b, branch + 1, last_b[leg])
         last_c[leg] = jnp.where(is_b, last_c[leg], branch + 1)
 
-    block = lax.broadcasted_iota(jnp.int32, (part, inner), 1) // width
+    block = lax.broadcasted_iota(jnp.int32, (stripe, inner), 1) // width
 
     def apply_leg(values, wide):
         product = dot(values, wide)
@@ -249,7 +252,7 @@
             for comp in range(2):
                 taken = None
                 for t in range(peers):
-                    tile = product[t * part : (t + 1) * part, comp * inner : (comp + 1) * inner]
+                    tile = product[t * stripe : (t + 1) * stripe, comp * inner : (comp + 1) * inner]
                     shift = (t - m) * width % inner
                     if shift:
                         tile = pltpu.roll(tile, shift, 1)
@@ -280,35 +283,36 @@
     for leg in range(legs):
         top = past[leg, last_c[leg]]
         wides.append(wide_of(top if leg < early else scaled(top)))
-    from_x(0)
     load_own.wait()
-    for copy in first:
-        copy.wait()
-    values = jnp.concatenate(
-        [jnp.concatenate([got[m, 0], got[m, 1]], axis=1) for m in range(peers)], axis=0
-    )
-    values = apply_leg(values, wides[0])
-    from_x(1)
-    for leg in range(1, legs - 1):
-        values = apply_leg(values, wides[leg])
-    from_x(2)
-    values = apply_leg(values, wides[legs - 1])
-    for m in range(peers):
-        leave[m] = values[m * part : (m + 1) * part]
-
     last = []
-    for step in range(1, peers):
-        target = lax.rem(me + step, peers)
-        copy = pltpu.make_async_remote_copy(
-            src_ref=leave.at[target],
-            dst_ref=back.at[me],
-            send_sem=last_send.at[step - 1],
-            recv_sem=last_recv.at[step - 1],
-            device_id={"modes": target},
-            device_id_type=MESH,
+    for wave in range(WAVES):
+        strip = pl.ds(wave * stripe, stripe)
+        for copy in first[wave * (peers - 1) : (wave + 1) * (peers - 1)]:
+            copy.wait()
+        from_x(wave)
+        values = jnp.concatenate(
+            [
+                jnp.concatenate([got[m, 0, strip, :], got[m, 1, strip, :]], axis=1)
+                for m in range(peers)
+            ],
+            axis=0,
         )
-        copy.start()
-        last.append(copy)
+        for leg in range(legs):
+            values = apply_leg(values, wides[leg])
+        for m in range(peers):
+            leave[m, strip, :] = values[m * stripe : (m + 1) * stripe]
+        for step in range(1, peers):
+            target = lax.rem(me + step, peers)
+            copy = pltpu.make_async_remote_copy(
+                src_ref=leave.at[target, strip, :],
+                dst_ref=back.at[me, strip, :],
+                send_sem=last_send.at[wave, step - 1],
+                recv_sem=last_recv.at[wave, step - 1],
+                device_id={"modes": target},
+                device_id_type=MESH,
+            )
+            copy.start()
+            last.append(copy)
     back[me] = leave[me]
 
     factors = [past[leg, last_b[leg]] for leg in range(legs)]
@@ -336,11 +340,9 @@
         ],
         axis=0,
     )
-    from_y(0)
-    from_x(3)
-    from_y(1)
-    from_x(4)
-    from_y(2)
+    for chunk in range(WAVES, DIRECT - 1):
+        from_x(chunk)
+        from_y(chunk - WAVES)
 
     for copy in last:
         copy.wait()
@@ -397,6 +399,9 @@
     real_sum, imag_sum = project(home, real_sum, imag_sum)
     own.wait()
     real_sum, imag_sum = project(sibling, real_sum, imag_sum)
+    from_x(DIRECT - 1)
+    for chunk in range(DIRECT - 1 - WAVES, handed):
+        from_y(chunk)
     real_sum, imag_sum = project(across, real_sum, imag_sum)
     for copy in over_core:
         copy.wait()
@@ -404,8 +409,8 @@
     for gain in [jnp.minimum(g, 1.0) for g in gains] + [jnp.maximum(g, 1.0) for g in gains]:
         real_sum = real_sum * gain
         imag_sum = imag_sum * gain
-    out_ref[0] = real_sum
-    out_ref[1] = imag_sum
+    out_ref[0] = real_sum.astype(jnp.bfloat16)
+    out_ref[1] = imag_sum.astype(jnp.bfloat16)
     for copy in over_x:
         copy.wait_send()
     for copy in over_y:
@@ -424,7 +429,7 @@
     whole = pl.BlockSpec(memory_space=pl.ANY)
     result = pl.pallas_call(
         functools.partial(fused, (peers, legs, branches, slabs, inner, depth)),
-        out_shape=jax.ShapeDtypeStruct((2, row_total, out_len), jnp.float32),
+        out_shape=jax.ShapeDtypeStruct((2, row_total, out_len), bf16),
         in_specs=[
             whole,
             whole,
@@ -443,10 +448,10 @@
             pltpu.VMEM((peers, part, 2 * inner), bf16),
             pltpu.VMEM((lax.axis_size("half"), 2, depth, out_len), bf16),
             pltpu.SemaphoreType.DMA((4 + legs,)),
-            pltpu.SemaphoreType.DMA((peers - 1,)),
-            pltpu.SemaphoreType.DMA((peers - 1,)),
-            pltpu.SemaphoreType.DMA((peers - 1,)),
-            pltpu.SemaphoreType.DMA((peers - 1,)),
+            pltpu.SemaphoreType.DMA((WAVES, peers - 1)),
+            pltpu.SemaphoreType.DMA((WAVES, peers - 1)),
+            pltpu.SemaphoreType.DMA((WAVES, peers - 1)),
+            pltpu.SemaphoreType.DMA((WAVES, peers - 1)),
             pltpu.SemaphoreType.DMA((DIRECT,)),
             pltpu.SemaphoreType.DMA((DIRECT,)),
             pltpu.SemaphoreType.DMA((CHUNKS - DIRECT,)),
@@ -464,7 +469,7 @@
         out_proj.reshape(out_proj.shape[1:]),
         groups.reshape(1, row_total),
     )
-    return result.astype(bf16).reshape(1, 1, 2, row_total, out_len)
+    return result.reshape(1, 1, 2, row_total, out_len)
 
 
 def solution(mesh):

time: 20.5 us -> 20.7 us (level)
  other arithmetic: 1.54 us -> 0 us
  local copies, waits for them, and re-layouts: 0 us -> 1.47 us
    reshape x1 -> x0, other arithmetic: 1.54 us -> none  [local(): return result.astype(bf16).reshape(1, 1, 2, row_total, out_len)]
    unnamed x0 -> x1, local copies, waits for them, and re-layouts: none -> 1.47 us
where the time goes in v5:
time: 20.7 us; the launch traced here: 20.5 us
  Pallas kernels  19 us (92%)
  local copies, waits for them, and re-layouts  1.47 us (7%)
    pallas_call x1, Pallas kernels, local(): pl.pallas_call(functools.partial(fused, (peers, legs, branches, slabs, in...  19 us
    unnamed x1, local copies, waits for them, and re-layouts  1.47 us

profile of v5, /device:TPU:0, one launch (start us, length us, event | category | flops | bytes accessed | tf_op | source)
XLA Modules:
  0.0 20.5 jit_solution(3718794268690690203)
XLA Ops:
  0.0 19.0 %shard_map.55 = bf16[2,64,256]{2,1,0:T(8,128)(2,1)} custom-call(bf16[2,256,128]{2,1,0:T(8,128)(2,1)} %bitcast.6, bf16[4,6,2,128,128]{4,3,2,1,0:T(8,128)(2,1)} %mats_hbm.1, s32[4,6]{1,0:T(4,128)} %modes_hbm.1, bf16[2,512,256]{2,1,0:T(8,128)(2,1)} %bitcast.4, s32[1,64]{1,0:T(1,128)} %bitcast.7), custom_call_target="tpu_custom_call" | custom-call | tf_op jit(solution)/shard_map/pallas_call | solution.py:430
  19.0 1.5 %copy.7 = bf16[1,1,2,64,256]{4,3,2,1,0:T(8,128)(2,1)} copy(bf16[1,1,2,64,256]{4,3,2,1,0:T(8,128)(2,1)} %bitcast.5) | data formatting | bytes 131072

commit v6 on v5

--- a/solution.py
+++ b/solution.py
@@ -8,8 +8,8 @@
 from jax.sharding import PartitionSpec as P
 
 MESH = pl.DeviceIdType.MESH
-CHUNKS = 8
-DIRECT = 5
+CHUNKS = 16
+DIRECT = 9
 WAVES = 2
 
 
@@ -276,6 +276,7 @@
             for leg in group:
                 next_branch(leg, branch)
         if group[0] == 0:
+            from_x(0)
             own.start()
             load_proj.start()
             load_groups.start()
@@ -283,13 +284,13 @@
     for leg in range(legs):
         top = past[leg, last_c[leg]]
         wides.append(wide_of(top if leg < early else scaled(top)))
+    from_x(1)
     load_own.wait()
     last = []
     for wave in range(WAVES):
         strip = pl.ds(wave * stripe, stripe)
         for copy in first[wave * (peers - 1) : (wave + 1) * (peers - 1)]:
             copy.wait()
-        from_x(wave)
         values = jnp.concatenate(
             [
                 jnp.concatenate([got[m, 0, strip, :], got[m, 1, strip, :]], axis=1)
@@ -299,6 +300,10 @@
         )
         for leg in range(legs):
             values = apply_leg(values, wides[leg])
+            if leg == legs // 2 - 1:
+                from_x(2 + 2 * wave)
+                if wave:
+                    from_y(1)
         for m in range(peers):
             leave[m, strip, :] = values[m * stripe : (m + 1) * stripe]
         for step in range(1, peers):
@@ -313,6 +318,8 @@
             )
             copy.start()
             last.append(copy)
+        from_x(3 + 2 * wave)
+        from_y(2 * wave)
     back[me] = leave[me]
 
     factors = [past[leg, last_b[leg]] for leg in range(legs)]
@@ -340,10 +347,11 @@
         ],
         axis=0,
     )
-    for chunk in range(WAVES, DIRECT - 1):
-        from_x(chunk)
-        from_y(chunk - WAVES)
-
+    from_x(6)
+    from_y(3)
+    from_y(4)
+    from_x(7)
+    from_y(5)
     for copy in last:
         copy.wait()
     arrived = jnp.concatenate([back[m] for m in range(peers)], axis=0)
@@ -395,13 +403,12 @@
         imag_sum = jnp.where(here, by_imag[:count] + by_real[count:], imag_sum)
         return real_sum, imag_sum
 
+    from_x(8)
+    from_y(6)
     load_proj.wait()
     real_sum, imag_sum = project(home, real_sum, imag_sum)
     own.wait()
     real_sum, imag_sum = project(sibling, real_sum, imag_sum)
-    from_x(DIRECT - 1)
-    for chunk in range(DIRECT - 1 - WAVES, handed):
-        from_y(chunk)
     real_sum, imag_sum = project(across, real_sum, imag_sum)
     for copy in over_core:
         copy.wait()

time: 20.7 us -> 21.6 us (1.043)
  Pallas kernels: 19 us -> 19.9 us
    pallas_call x1, Pallas kernels: 19 us -> 19.9 us  [local(): pl.pallas_call(functools.partial(fused, (peers, legs, branches, slabs, in...]
where the time goes in v6:
time: 21.6 us; the launch traced here: 21.4 us
  Pallas kernels  19.9 us (92%)
  local copies, waits for them, and re-layouts  1.47 us (7%)
    pallas_call x1, Pallas kernels, local(): pl.pallas_call(functools.partial(fused, (peers, legs, branches, slabs, in...  19.9 us
    unnamed x1, local copies, waits for them, and re-layouts  1.47 us

profile of v6, /device:TPU:0, one launch (start us, length us, event | category | flops | bytes accessed | tf_op | source)
XLA Modules:
  0.0 21.4 jit_solution(17670408749822441157)
XLA Ops:
  0.0 19.9 %shard_map.55 = bf16[2,64,256]{2,1,0:T(8,128)(2,1)} custom-call(bf16[2,256,128]{2,1,0:T(8,128)(2,1)} %bitcast.6, bf16[4,6,2,128,128]{4,3,2,1,0:T(8,128)(2,1)} %mats_hbm.1, s32[4,6]{1,0:T(4,128)} %modes_hbm.1, bf16[2,512,256]{2,1,0:T(8,128)(2,1)} %bitcast.4, s32[1,64]{1,0:T(1,128)} %bitcast.7), custom_call_target="tpu_custom_call" | custom-call | tf_op jit(solution)/shard_map/pallas_call | solution.py:437
  20.0 1.5 %copy.7 = bf16[1,1,2,64,256]{4,3,2,1,0:T(8,128)(2,1)} copy(bf16[1,1,2,64,256]{4,3,2,1,0:T(8,128)(2,1)} %bitcast.5) | data formatting | bytes 131072

commit v7 on v4

--- a/solution.py
+++ b/solution.py
@@ -224,9 +224,9 @@
 
     def start_leg(leg):
         load_mats[leg].wait()
-        past[leg, 0] = identity
-        past[leg, 1, :, :inner] = mats[leg, 0, 0]
-        past[leg, 1, :, inner:] = mats[leg, 0, 1]
+        past[leg][0] = identity
+        past[leg][1, :, :inner] = mats[leg, 0, 0]
+        past[leg][1, :, inner:] = mats[leg, 0, 1]
         is_b = modes_ref[leg, 0] == 0
         last_b[leg] = jnp.where(is_b, 1, 0)
         last_c[leg] = jnp.where(is_b, 0, 1)
@@ -234,8 +234,8 @@
     def next_branch(leg, branch):
         is_b = modes_ref[leg, branch] == 0
         top = jnp.concatenate([mats[leg, branch, 0], mats[leg, branch, 1]], axis=1)
-        before = past[leg, jnp.where(is_b, last_b[leg], last_c[leg])]
-        past[leg, branch + 1] = dot(before, wide_of(top)).astype(jnp.bfloat16)
+        before = past[leg][jnp.where(is_b, last_b[leg], last_c[leg])]
+        past[leg][branch + 1] = dot(before, wide_of(top)).astype(jnp.bfloat16)
         last_b[leg] = jnp.where(is_b, branch + 1, last_b[leg])
         last_c[leg] = jnp.where(is_b, last_c[leg], branch + 1)
 
@@ -266,19 +266,17 @@
         return top.astype(jnp.bfloat16)
 
     early = min(2, legs)
-    for group in (range(early), range(early, legs)):
-        for leg in group:
-            start_leg(leg)
-        for branch in range(1, branches):
-            for leg in group:
-                next_branch(leg, branch)
-        if group[0] == 0:
-            own.start()
-            load_proj.start()
-            load_groups.start()
+    for leg in range(legs):
+        start_leg(leg)
+    for branch in range(1, branches):
+        for leg in range(legs):
+            next_branch(leg, branch)
+    own.start()
+    load_proj.start()
+    load_groups.start()
     wides = []
     for leg in range(legs):
-        top = past[leg, last_c[leg]]
+        top = past[leg][last_c[leg]]
         wides.append(wide_of(top if leg < early else scaled(top)))
     from_x(0)
     load_own.wait()
@@ -311,7 +309,7 @@
         last.append(copy)
     back[me] = leave[me]
 
-    factors = [past[leg, last_b[leg]] for leg in range(legs)]
+    factors = [past[leg][last_b[leg]] for leg in range(legs)]
     while len(factors) > 1:
         pairs = [
             scaled(dot(factors[i], wide_of(factors[i + 1]))) for i in range(0, len(factors) - 1, 2)
@@ -404,8 +402,8 @@
     for gain in [jnp.minimum(g, 1.0) for g in gains] + [jnp.maximum(g, 1.0) for g in gains]:
         real_sum = real_sum * gain
         imag_sum = imag_sum * gain
-    out_ref[0] = real_sum
-    out_ref[1] = imag_sum
+    out_ref[0] = real_sum.astype(jnp.bfloat16)
+    out_ref[1] = imag_sum.astype(jnp.bfloat16)
     for copy in over_x:
         copy.wait_send()
     for copy in over_y:
@@ -424,7 +422,7 @@
     whole = pl.BlockSpec(memory_space=pl.ANY)
     result = pl.pallas_call(
         functools.partial(fused, (peers, legs, branches, slabs, inner, depth)),
-        out_shape=jax.ShapeDtypeStruct((2, row_total, out_len), jnp.float32),
+        out_shape=jax.ShapeDtypeStruct((2, row_total, out_len), bf16),
         in_specs=[
             whole,
             whole,
@@ -437,7 +435,7 @@
             pltpu.SMEM(branch_modes.shape, jnp.int32),
             pltpu.VMEM((1, row_total), jnp.int32),
             pltpu.VMEM(branch_mats.shape, bf16),
-            pltpu.VMEM((legs, branches + 1, inner, 2 * inner), bf16),
+            [pltpu.VMEM((branches + 1, inner, 2 * inner), bf16)] * legs,
             pltpu.VMEM((peers, 2, part, inner), bf16),
             pltpu.VMEM((peers, part, 2 * inner), bf16),
             pltpu.VMEM((peers, part, 2 * inner), bf16),
@@ -464,7 +462,7 @@
         out_proj.reshape(out_proj.shape[1:]),
         groups.reshape(1, row_total),
     )
-    return result.astype(bf16).reshape(1, 1, 2, row_total, out_len)
+    return result.reshape(1, 1, 2, row_total, out_len)
 
 
 def solution(mesh):

time: 20.5 us -> 20.5 us (level)
  other arithmetic: 1.54 us -> 0 us
  local copies, waits for them, and re-layouts: 0 us -> 1.47 us
    reshape x1 -> x0, other arithmetic: 1.54 us -> none  [local(): return result.astype(bf16).reshape(1, 1, 2, row_total, out_len)]
    unnamed x0 -> x1, local copies, waits for them, and re-layouts: none -> 1.47 us
where the time goes in v7:
time: 20.5 us; the launch traced here: 20.3 us
  Pallas kernels  18.8 us (92%)
  local copies, waits for them, and re-layouts  1.47 us (7%)
    pallas_call x1, Pallas kernels, local(): pl.pallas_call(functools.partial(fused, (peers, legs, branches, slabs, in...  18.8 us
    unnamed x1, local copies, waits for them, and re-layouts  1.47 us

profile of v7, /device:TPU:0, one launch (start us, length us, event | category | flops | bytes accessed | tf_op | source)
XLA Modules:
  0.0 20.3 jit_solution(15792638983321683056)
XLA Ops:
  0.0 18.8 %shard_map.55 = bf16[2,64,256]{2,1,0:T(8,128)(2,1)} custom-call(bf16[2,256,128]{2,1,0:T(8,128)(2,1)} %bitcast.6, bf16[4,6,2,128,128]{4,3,2,1,0:T(8,128)(2,1)} %mats_hbm.1, s32[4,6]{1,0:T(4,128)} %modes_hbm.1, bf16[2,512,256]{2,1,0:T(8,128)(2,1)} %bitcast.4, s32[1,64]{1,0:T(1,128)} %bitcast.7), custom_call_target="tpu_custom_call" | custom-call | tf_op jit(solution)/shard_map/pallas_call | solution.py:423
  18.8 1.5 %copy.7 = bf16[1,1,2,64,256]{4,3,2,1,0:T(8,128)(2,1)} copy(bf16[1,1,2,64,256]{4,3,2,1,0:T(8,128)(2,1)} %bitcast.5) | data formatting | bytes 131072

commit v8 on v5

--- a/solution.py
+++ b/solution.py
@@ -227,9 +227,9 @@
 
     def start_leg(leg):
         load_mats[leg].wait()
-        past[leg, 0] = identity
-        past[leg, 1, :, :inner] = mats[leg, 0, 0]
-        past[leg, 1, :, inner:] = mats[leg, 0, 1]
+        past[leg][0] = identity
+        past[leg][1, :, :inner] = mats[leg, 0, 0]
+        past[leg][1, :, inner:] = mats[leg, 0, 1]
         is_b = modes_ref[leg, 0] == 0
         last_b[leg] = jnp.where(is_b, 1, 0)
         last_c[leg] = jnp.where(is_b, 0, 1)
@@ -237,8 +237,8 @@
     def next_branch(leg, branch):
         is_b = modes_ref[leg, branch] == 0
         top = jnp.concatenate([mats[leg, branch, 0], mats[leg, branch, 1]], axis=1)
-        before = past[leg, jnp.where(is_b, last_b[leg], last_c[leg])]
-        past[leg, branch + 1] = dot(before, wide_of(top)).astype(jnp.bfloat16)
+        before = past[leg][jnp.where(is_b, last_b[leg], last_c[leg])]
+        past[leg][branch + 1] = dot(before, wide_of(top)).astype(jnp.bfloat16)
         last_b[leg] = jnp.where(is_b, branch + 1, last_b[leg])
         last_c[leg] = jnp.where(is_b, last_c[leg], branch + 1)
 
@@ -269,19 +269,17 @@
         return top.astype(jnp.bfloat16)
 
     early = min(2, legs)
-    for group in (range(early), range(early, legs)):
-        for leg in group:
-            start_leg(leg)
-        for branch in range(1, branches):
-            for leg in group:
-                next_branch(leg, branch)
-        if group[0] == 0:
-            own.start()
-            load_proj.start()
-            load_groups.start()
+    for leg in range(legs):
+        start_leg(leg)
+    for branch in range(1, branches):
+        for leg in range(legs):
+            next_branch(leg, branch)
+    own.start()
+    load_proj.start()
+    load_groups.start()
     wides = []
     for leg in range(legs):
-        top = past[leg, last_c[leg]]
+        top = past[leg][last_c[leg]]
         wides.append(wide_of(top if leg < early else scaled(top)))
     load_own.wait()
     last = []
@@ -315,7 +313,7 @@
             last.append(copy)
     back[me] = leave[me]
 
-    factors = [past[leg, last_b[leg]] for leg in range(legs)]
+    factors = [past[leg][last_b[leg]] for leg in range(legs)]
     while len(factors) > 1:
         pairs = [
             scaled(dot(factors[i], wide_of(factors[i + 1]))) for i in range(0, len(factors) - 1, 2)
@@ -395,13 +393,13 @@
         imag_sum = jnp.where(here, by_imag[:count] + by_real[count:], imag_sum)
         return real_sum, imag_sum
 
+    from_x(DIRECT - 1)
+    for chunk in range(DIRECT - 1 - WAVES, handed):
+        from_y(chunk)
     load_proj.wait()
     real_sum, imag_sum = project(home, real_sum, imag_sum)
     own.wait()
     real_sum, imag_sum = project(sibling, real_sum, imag_sum)
-    from_x(DIRECT - 1)
-    for chunk in range(DIRECT - 1 - WAVES, handed):
-        from_y(chunk)
     real_sum, imag_sum = project(across, real_sum, imag_sum)
     for copy in over_core:
         copy.wait()
@@ -442,7 +440,7 @@
             pltpu.SMEM(branch_modes.shape, jnp.int32),
             pltpu.VMEM((1, row_total), jnp.int32),
             pltpu.VMEM(branch_mats.shape, bf16),
-            pltpu.VMEM((legs, branches + 1, inner, 2 * inner), bf16),
+            [pltpu.VMEM((branches + 1, inner, 2 * inner), bf16)] * legs,
             pltpu.VMEM((peers, 2, part, inner), bf16),
             pltpu.VMEM((peers, part, 2 * inner), bf16),
             pltpu.VMEM((peers, part, 2 * inner), bf16),

time: 20.7 us -> 20.7 us (level)
  no operation moved by 1% of the time
where the time goes in v8:
time: 20.7 us; the launch traced here: 20.5 us
  Pallas kernels  19 us (92%)
  local copies, waits for them, and re-layouts  1.47 us (7%)
    pallas_call x1, Pallas kernels, local(): pl.pallas_call(functools.partial(fused, (peers, legs, branches, slabs, in...  19 us
    unnamed x1, local copies, waits for them, and re-layouts  1.47 us

profile of v8, /device:TPU:0, one launch (start us, length us, event | category | flops | bytes accessed | tf_op | source)
XLA Modules:
  0.0 20.5 jit_solution(7036662464644090363)
XLA Ops:
  0.0 19.0 %shard_map.55 = bf16[2,64,256]{2,1,0:T(8,128)(2,1)} custom-call(bf16[2,256,128]{2,1,0:T(8,128)(2,1)} %bitcast.6, bf16[4,6,2,128,128]{4,3,2,1,0:T(8,128)(2,1)} %mats_hbm.1, s32[4,6]{1,0:T(4,128)} %modes_hbm.1, bf16[2,512,256]{2,1,0:T(8,128)(2,1)} %bitcast.4, s32[1,64]{1,0:T(1,128)} %bitcast.7), custom_call_target="tpu_custom_call" | custom-call | tf_op jit(solution)/shard_map/pallas_call | solution.py:428
  19.0 1.5 %copy.7 = bf16[1,1,2,64,256]{4,3,2,1,0:T(8,128)(2,1)} copy(bf16[1,1,2,64,256]{4,3,2,1,0:T(8,128)(2,1)} %bitcast.5) | data formatting | bytes 131072

commit v9 on v8

--- a/solution.py
+++ b/solution.py
@@ -145,6 +145,22 @@
     load_own.start()
     pl.semaphore_wait(barrier, peers + 2)
 
+    def rows_of(which, chunk):
+        forward = pl.multiple_of(which * (CHUNKS - 1) * piece + (1 - 2 * which) * chunk * piece, piece)
+        return pl.ds(forward, piece)
+
+    over_x, over_y, over_core = [], [], []
+    for chunk in range(DIRECT):
+        copy = pltpu.make_async_remote_copy(
+            src_ref=proj_ref.at[:, rows_of(row, chunk), :],
+            dst_ref=weights.at[home, :, rows_of(row, chunk), :],
+            send_sem=x_send.at[chunk],
+            recv_sem=x_recv.at[chunk],
+            device_id={"half": across},
+            device_id_type=MESH,
+        )
+        copy.start()
+        over_x.append(copy)
     stripe = part // WAVES
     first = []
     for wave in range(WAVES):
@@ -161,22 +177,6 @@
             copy.start()
             first.append(copy)
 
-    def rows_of(which, chunk):
-        forward = pl.multiple_of(which * (CHUNKS - 1) * piece + (1 - 2 * which) * chunk * piece, piece)
-        return pl.ds(forward, piece)
-
-    over_x, over_y, over_core = [], [], []
-    for chunk in range(DIRECT):
-        copy = pltpu.make_async_remote_copy(
-            src_ref=proj_ref.at[:, rows_of(row, chunk), :],
-            dst_ref=weights.at[home, :, rows_of(row, chunk), :],
-            send_sem=x_send.at[chunk],
-            recv_sem=x_recv.at[chunk],
-            device_id={"half": across},
-            device_id_type=MESH,
-        )
-        copy.start()
-        over_x.append(copy)
     own = pltpu.make_async_remote_copy(
         src_ref=proj_ref,
         dst_ref=weights.at[home],
@@ -281,13 +281,13 @@
     for leg in range(legs):
         top = past[leg][last_c[leg]]
         wides.append(wide_of(top if leg < early else scaled(top)))
+    from_x(0)
     load_own.wait()
     last = []
     for wave in range(WAVES):
         strip = pl.ds(wave * stripe, stripe)
         for copy in first[wave * (peers - 1) : (wave + 1) * (peers - 1)]:
             copy.wait()
-        from_x(wave)
         values = jnp.concatenate(
             [
                 jnp.concatenate([got[m, 0, strip, :], got[m, 1, strip, :]], axis=1)
@@ -297,6 +297,8 @@
         )
         for leg in range(legs):
             values = apply_leg(values, wides[leg])
+            if wave == WAVES - 1 and leg == 0:
+                from_x(2)
         for m in range(peers):
             leave[m, strip, :] = values[m * stripe : (m + 1) * stripe]
         for step in range(1, peers):
@@ -311,6 +313,8 @@
             )
             copy.start()
             last.append(copy)
+        if wave == 0:
+            from_x(1)
     back[me] = leave[me]
 
     factors = [past[leg][last_b[leg]] for leg in range(legs)]
@@ -338,9 +342,10 @@
         ],
         axis=0,
     )
-    for chunk in range(WAVES, DIRECT - 1):
-        from_x(chunk)
-        from_y(chunk - WAVES)
+    for chunk in range(handed):
+        from_y(chunk)
+        if chunk + handed < DIRECT:
+            from_x(chunk + handed)
 
     for copy in last:
         copy.wait()
@@ -393,9 +398,6 @@
         imag_sum = jnp.where(here, by_imag[:count] + by_real[count:], imag_sum)
         return real_sum, imag_sum
 
-    from_x(DIRECT - 1)
-    for chunk in range(DIRECT - 1 - WAVES, handed):
-        from_y(chunk)
     load_proj.wait()
     real_sum, imag_sum = project(home, real_sum, imag_sum)
     own.wait()

time: 20.7 us -> 20.5 us (level)
  no operation moved by 1% of the time
where the time goes in v9:
time: 20.5 us; the launch traced here: 20.4 us
  Pallas kernels  18.9 us (92%)
  local copies, waits for them, and re-layouts  1.47 us (7%)
    pallas_call x1, Pallas kernels, local(): pl.pallas_call(functools.partial(fused, (peers, legs, branches, slabs, in...  18.9 us
    unnamed x1, local copies, waits for them, and re-layouts  1.47 us

profile of v9, /device:TPU:0, one launch (start us, length us, event | category | flops | bytes accessed | tf_op | source)
XLA Modules:
  0.0 20.4 jit_solution(1962648212744624364)
XLA Ops:
  0.0 18.9 %shard_map.55 = bf16[2,64,256]{2,1,0:T(8,128)(2,1)} custom-call(bf16[2,256,128]{2,1,0:T(8,128)(2,1)} %bitcast.6, bf16[4,6,2,128,128]{4,3,2,1,0:T(8,128)(2,1)} %mats_hbm.1, s32[4,6]{1,0:T(4,128)} %modes_hbm.1, bf16[2,512,256]{2,1,0:T(8,128)(2,1)} %bitcast.4, s32[1,64]{1,0:T(1,128)} %bitcast.7), custom_call_target="tpu_custom_call" | custom-call | tf_op jit(solution)/shard_map/pallas_call | solution.py:430
  18.9 1.5 %copy.7 = bf16[1,1,2,64,256]{4,3,2,1,0:T(8,128)(2,1)} copy(bf16[1,1,2,64,256]{4,3,2,1,0:T(8,128)(2,1)} %bitcast.5) | data formatting | bytes 131072

commit v10 on v9

--- a/solution.py
+++ b/solution.py
@@ -288,6 +288,8 @@
         strip = pl.ds(wave * stripe, stripe)
         for copy in first[wave * (peers - 1) : (wave + 1) * (peers - 1)]:
             copy.wait()
+        if wave == WAVES - 1:
+            from_x(1)
         values = jnp.concatenate(
             [
                 jnp.concatenate([got[m, 0, strip, :], got[m, 1, strip, :]], axis=1)
@@ -297,8 +299,6 @@
         )
         for leg in range(legs):
             values = apply_leg(values, wides[leg])
-            if wave == WAVES - 1 and leg == 0:
-                from_x(2)
         for m in range(peers):
             leave[m, strip, :] = values[m * stripe : (m + 1) * stripe]
         for step in range(1, peers):
@@ -313,8 +313,7 @@
             )
             copy.start()
             last.append(copy)
-        if wave == 0:
-            from_x(1)
+    from_x(2)
     back[me] = leave[me]
 
     factors = [past[leg][last_b[leg]] for leg in range(legs)]
@@ -342,10 +341,9 @@
         ],
         axis=0,
     )
-    for chunk in range(handed):
-        from_y(chunk)
-        if chunk + handed < DIRECT:
-            from_x(chunk + handed)
+    from_y(0)
+    from_x(3)
+    from_y(1)
 
     for copy in last:
         copy.wait()
@@ -398,6 +396,8 @@
         imag_sum = jnp.where(here, by_imag[:count] + by_real[count:], imag_sum)
         return real_sum, imag_sum
 
+    from_x(4)
+    from_y(2)
     load_proj.wait()
     real_sum, imag_sum = project(home, real_sum, imag_sum)
     own.wait()

time: 20.5 us -> 20.3 us (level)
    pallas_call x1, Pallas kernels: 18.9 us -> 18.7 us  [local(): pl.pallas_call(functools.partial(fused, (peers, legs, branches, slabs, in...]
where the time goes in v10:
time: 20.3 us; the launch traced here: 20.2 us
  Pallas kernels  18.7 us (92%)
  local copies, waits for them, and re-layouts  1.47 us (7%)
    pallas_call x1, Pallas kernels, local(): pl.pallas_call(functools.partial(fused, (peers, legs, branches, slabs, in...  18.7 us
    unnamed x1, local copies, waits for them, and re-layouts  1.47 us

profile of v10, /device:TPU:0, one launch (start us, length us, event | category | flops | bytes accessed | tf_op | source)
XLA Modules:
  0.0 20.2 jit_solution(17157456617417903296)
XLA Ops:
  0.0 18.7 %shard_map.55 = bf16[2,64,256]{2,1,0:T(8,128)(2,1)} custom-call(bf16[2,256,128]{2,1,0:T(8,128)(2,1)} %bitcast.6, bf16[4,6,2,128,128]{4,3,2,1,0:T(8,128)(2,1)} %mats_hbm.1, s32[4,6]{1,0:T(4,128)} %modes_hbm.1, bf16[2,512,256]{2,1,0:T(8,128)(2,1)} %bitcast.4, s32[1,64]{1,0:T(1,128)} %bitcast.7), custom_call_target="tpu_custom_call" | custom-call | tf_op jit(solution)/shard_map/pallas_call | solution.py:430
  18.7 1.5 %copy.7 = bf16[1,1,2,64,256]{4,3,2,1,0:T(8,128)(2,1)} copy(bf16[1,1,2,64,256]{4,3,2,1,0:T(8,128)(2,1)} %bitcast.5) | data formatting | bytes 131072
